TPU v7x, 256 devices: a whole 4x4x8 slice. The times are simulated.
256 devices in a mesh: dp: 16 (over x_hi, y, core), seq: 16 (over z, x_lo).
Axes of the slice: x: 4 (x_hi: 2, x_lo: 2; x = x_hi * 2 + x_lo), y: 4, z: 8, core: 2. Of those that a mesh axis runs over, the one named last changes fastest.
Arguments:
- query_states: bfloat16 [16, 2048, 2048], P('dp', 'seq'), may hold values from -45 to 45
- key_states: bfloat16 [16, 2048, 2048], P('dp', 'seq'), may hold values from -30 to 30
- value_states: bfloat16 [16, 2048, 2048], P('dp', 'seq'), may hold values from -6 to 6
- out_grad: bfloat16 [16, 2048, 2048], P('dp', 'seq'), may hold values from -6 to 6
- doc_ids: int32 [16, 2048], P('dp', 'seq'), may hold values from 0 to 7, never falling along the last dimension, each value on 1 to 512 neighbouring positions
- query_gain: float32 [2048], replicated, may hold values from 0.375 to 6.25
- key_gain: float32 [2048], replicated, may hold values from 0.375 to 6.25
Outputs:
- query_grad: bfloat16 [16, 2048, 2048], P('dp', 'seq')
- key_grad: bfloat16 [16, 2048, 2048], P('dp', 'seq')
- value_grad: bfloat16 [16, 2048, 2048], P('dp', 'seq')
- query_gain_grad: float32 [2048], P('seq')
- key_gain_grad: float32 [2048], P('seq')
Inputs may be any that keep to these rules, and one draw needn't show every extreme that they name: `doc_ids`: Non-decreasing along each sequence; each document holds 1 to 512 positions, one exactly that many.
All inputs are finite; a program needn't handle non-finite values.
Results may differ from a plain program's by a relative error of at most 0.012.
The roundings to bfloat16 on the way count: a program that leaves them out, or rounds other values in their place, can miss the bound.
Values may be sent and summed in bfloat16 or wider, within the bound.
A program may use at most 64 MiB of HBM per device.

v0:
```python
import jax
import jax.numpy as jnp
from jax import lax
from jax.sharding import PartitionSpec as P

HD = 128


EPS = 1e-06
MASKED = -1e30


def normalize(values, norm_gain_weight):
    input_float_rows = values.astype(jnp.float32)
    inverse_root_mean = lax.rsqrt(
        jnp.mean(input_float_rows * input_float_rows, axis=-1, keepdims=True) + EPS
    )
    normalized_input = input_float_rows * inverse_root_mean
    return (
        normalized_input,
        inverse_root_mean,
        (normalized_input * norm_gain_weight).astype(jnp.bfloat16),
    )


def norm_backward_pass(normalized_input, inverse_root_mean, norm_gain_weight, incoming_gradient):
    gain_scaled_gradient = incoming_gradient * norm_gain_weight
    input_gradient = inverse_root_mean * (
        gain_scaled_gradient
        - normalized_input
        * jnp.mean(gain_scaled_gradient * normalized_input, axis=-1, keepdims=True)
    )
    return (
        input_gradient.astype(jnp.bfloat16),
        jnp.sum(incoming_gradient * normalized_input, axis=0),
    )


def attend_back(q_norm, k_norm, values, dout, segs):
    seq_len, local_heads, head_dim = q_norm.shape
    block = min(512, seq_len)
    nblocks = seq_len // block
    scale = HD ** (-0.5)
    position = jnp.arange(seq_len, dtype=jnp.int32)

    def block_rows(array, index):
        return lax.dynamic_slice_in_dim(array, index * block, block, 0)

    def block_mask(query_idx, key_idx):
        q_pos = block_rows(position, query_idx)
        k_pos = block_rows(position, key_idx)
        q_seg = block_rows(segs, query_idx)
        k_seg = block_rows(segs, key_idx)
        return (k_pos[None, :] <= q_pos[:, None]) & (k_seg[None, :] == q_seg[:, None])

    def is_live(query_idx, key_idx):
        return (key_idx <= query_idx) & (
            segs[query_idx * block] <= segs[key_idx * block + block - 1]
        )

    def row_stats(query_idx):
        q_block = block_rows(q_norm, query_idx)
        d_block = block_rows(dout, query_idx)
        start = (
            jnp.full((local_heads, block), MASKED, jnp.float32),
            jnp.zeros((local_heads, block), jnp.float32),
            jnp.zeros((block, local_heads, head_dim), jnp.float32),
        )

        def add_key(key_idx, state):
            running_max, running_sum, weighted = state
            k_block = block_rows(k_norm, key_idx)
            v_block = block_rows(values, key_idx).astype(jnp.float32)
            allowed = block_mask(query_idx, key_idx)[None]
            scores = (
                jnp.einsum("qhd,khd->hqk", q_block, k_block, preferred_element_type=jnp.float32)
                * scale
            )
            scores = jnp.where(allowed, scores, MASKED)
            new_max = jnp.maximum(running_max, jnp.max(scores, axis=2))
            prob = jnp.where(allowed, jnp.exp(scores - new_max[:, :, None]), 0.0)
            fade = jnp.exp(running_max - new_max)
            running_sum = running_sum * fade + jnp.sum(prob, axis=2)
            weighted = weighted * fade.T[:, :, None] + jnp.einsum(
                "hqk,khd->qhd", prob, v_block, precision=lax.Precision.HIGHEST
            )
            return (new_max, running_sum, weighted)

        def row_guarded(key_idx, state):
            return lax.cond(
                is_live(query_idx, key_idx),
                lambda inner: add_key(key_idx, inner),
                lambda inner: inner,
                state,
            )

        running_max, running_sum, weighted = lax.fori_loop(0, query_idx + 1, row_guarded, start)
        lse = running_max + jnp.log(running_sum)
        attn = weighted / running_sum.T[:, :, None]
        delta = jnp.sum(d_block.astype(jnp.float32) * attn, axis=2).T
        return (lse, delta)

    lse_all, delta_all = lax.map(row_stats, jnp.arange(nblocks, dtype=jnp.int32))

    def key_block(dq_all, key_idx):
        k_block = block_rows(k_norm, key_idx)
        v_block = block_rows(values, key_idx)
        zeros_block = jnp.zeros((block, local_heads, head_dim), jnp.float32)

        def add_query(query_idx, state):
            dq_total, dk_acc, dv_acc = state
            q_block = block_rows(q_norm, query_idx)
            d_block = block_rows(dout, query_idx)
            allowed = block_mask(query_idx, key_idx)[None]
            scores = (
                jnp.einsum("qhd,khd->hqk", q_block, k_block, preferred_element_type=jnp.float32)
                * scale
            )
            prob = jnp.where(allowed, jnp.exp(scores - lse_all[query_idx][:, :, None]), 0.0)
            prob_low = prob.astype(jnp.bfloat16)
            dv_acc = dv_acc + jnp.einsum(
                "hqk,qhd->khd", prob_low, d_block, preferred_element_type=jnp.float32
            )
            dprob = jnp.einsum("qhd,khd->hqk", d_block, v_block, preferred_element_type=jnp.float32)
            dscore = (prob * (dprob - delta_all[query_idx][:, :, None]) * scale).astype(
                jnp.bfloat16
            )
            dq_part = jnp.einsum(
                "hqk,khd->qhd", dscore, k_block, preferred_element_type=jnp.float32
            )
            dq_total = lax.dynamic_update_slice_in_dim(
                dq_total, block_rows(dq_total, query_idx) + dq_part, query_idx * block, 0
            )
            dk_acc = dk_acc + jnp.einsum(
                "hqk,qhd->khd", dscore, q_block, preferred_element_type=jnp.float32
            )
            return (dq_total, dk_acc, dv_acc)

        start = (dq_all, zeros_block, zeros_block)

        def key_guarded(query_idx, state):
            return lax.cond(
                is_live(query_idx, key_idx),
                lambda inner: add_query(query_idx, inner),
                lambda inner: inner,
                state,
            )

        dq_all, dk_acc, dv_acc = lax.fori_loop(key_idx, nblocks, key_guarded, start)
        return (dq_all, (dk_acc, dv_acc.astype(jnp.bfloat16)))

    dq_norm, (dk_blocks, dv_blocks) = lax.scan(
        key_block,
        jnp.zeros((seq_len, local_heads, head_dim), jnp.float32),
        jnp.arange(nblocks, dtype=jnp.int32),
    )
    dk_norm = dk_blocks.reshape(seq_len, local_heads, head_dim)
    value_grad = dv_blocks.reshape(seq_len, local_heads, head_dim)
    return (dq_norm, dk_norm, value_grad)


def body(query_states, key_states, value_states, out_grad, doc_ids, query_gain, key_gain):
    tok_count = query_states.shape[1]
    feature = query_states.shape[2]
    groups = lax.axis_size("seq")
    width = feature // groups
    head_count = feature // HD
    mine = lax.axis_index("seq")
    gains_q = query_gain.reshape(head_count, HD)
    gains_k = key_gain.reshape(head_count, HD)
    q_hat_t, q_rec_t, q_normed_t = normalize(
        query_states[0].reshape(tok_count, head_count, HD), gains_q
    )
    k_hat_t, k_rec_t, k_normed_t = normalize(
        key_states[0].reshape(tok_count, head_count, HD), gains_k
    )
    first = q_normed_t.reshape(1, tok_count, feature)
    second = k_normed_t.reshape(1, tok_count, feature)
    packed_q = first.reshape(tok_count, groups, width)
    packed_k = second.reshape(tok_count, groups, width)
    packed_v = value_states.reshape(tok_count, groups, width)
    packed_d = out_grad.reshape(tok_count, groups, width)
    moved = (
        lax.all_to_all(packed_q, "seq", split_axis=1, concat_axis=0, tiled=True),
        lax.all_to_all(packed_k, "seq", split_axis=1, concat_axis=0, tiled=True),
        lax.all_to_all(packed_v, "seq", split_axis=1, concat_axis=0, tiled=True),
        lax.all_to_all(packed_d, "seq", split_axis=1, concat_axis=0, tiled=True),
    )
    heads_q, heads_k, heads_v, heads_d = [part for part in moved]
    segs = lax.all_gather(doc_ids, "seq", axis=1, tiled=True)[0]
    dq_norm, dk_norm, value_grad = attend_back(heads_q, heads_k, heads_v, heads_d, segs)
    back_norms = (
        lax.all_to_all(
            dq_norm.astype(jnp.bfloat16), "seq", split_axis=0, concat_axis=1, tiled=True
        ).astype(dq_norm.dtype),
        lax.all_to_all(
            dk_norm.astype(jnp.bfloat16), "seq", split_axis=0, concat_axis=1, tiled=True
        ).astype(dk_norm.dtype),
    )
    back_values = lax.all_to_all(value_grad, "seq", split_axis=0, concat_axis=1, tiled=True)
    query_grad, q_terms = norm_backward_pass(q_hat_t, q_rec_t, gains_q, back_norms[0])
    key_grad, k_terms = norm_backward_pass(k_hat_t, k_rec_t, gains_k, back_norms[1])
    q_total, k_total = lax.psum((q_terms.reshape(feature), k_terms.reshape(feature)), ("dp", "seq"))
    q_gain_grad = lax.dynamic_slice_in_dim(q_total, mine * width, width)
    k_gain_grad = lax.dynamic_slice_in_dim(k_total, mine * width, width)
    return (
        query_grad.reshape(1, tok_count, feature),
        key_grad.reshape(1, tok_count, feature),
        back_values.reshape(1, tok_count, feature),
        q_gain_grad,
        k_gain_grad,
    )


def solution(mesh):
    placed = (
        P("dp", "seq", None),
        P("dp", "seq", None),
        P("dp", "seq", None),
        P("dp", "seq", None),
        P("dp", "seq"),
        P(),
        P(),
    )
    return jax.shard_map(
        body,
        mesh=mesh,
        in_specs=placed,
        out_specs=(
            P("dp", "seq", None),
            P("dp", "seq", None),
            P("dp", "seq", None),
            P("seq"),
            P("seq"),
        ),
        check_vma=False,
    )
```

profile of v0, /device:TPU:1, one launch (start us, length us, event | category | flops | bytes accessed | tf_op | source)
XLA Modules:
  0.0 390.8 jit_solution(14319627387083906644)
XLA Ops:
  0.6 2.0 copy.59
  2.7 10.2 %all-to-all-start.1 = ((bf16[128,16,128]{0,2,1:T(8,128)(2,1)}), bf16[128,16,128]{0,2,1:T(8,128)(2,1)S(1)}, u32[]{:S(2)}, u32[]{:S(2)}) async-start(bf16[128,16,128]{0,2,1:T(8,128)(2,1)} %bitcast.30), calls=%async_computation.1 | async-start | bytes 1048576 | tf_op jit(solution)/shard_map/all_to_all | solution.py:186
  13.9 14.6 %all-to-all-done.1 = bf16[128,16,128]{0,2,1:T(8,128)(2,1)S(1)} async-done(((bf16[128,16,128]{0,2,1:T(8,128)(2,1)}), bf16[128,16,128]{0,2,1:T(8,128)(2,1)S(1)}, u32[]{:S(2)}, u32[]{:S(2)}) %all-to-all-start.1) | async-done | bytes 524320 | tf_op jit(solution)/shard_map/all_to_all | solution.py:186
  28.5 4.9 %all-to-all-start.3 = ((bf16[128,16,128]{0,2,1:T(8,128)(2,1)}), bf16[128,16,128]{0,2,1:T(8,128)(2,1)S(1)}, u32[]{:S(2)}, u32[]{:S(2)}) async-start(bf16[128,16,128]{0,2,1:T(8,128)(2,1)} %bitcast.39), calls=%async_computation.3 | async-start | bytes 1048576 | tf_op jit(solution)/shard_map/all_to_all | solution.py:187
  35.5 1.1 multiply_convert_fusion.1
  36.7 12.5 %all-to-all-done.3 = bf16[128,16,128]{0,2,1:T(8,128)(2,1)S(1)} async-done(((bf16[128,16,128]{0,2,1:T(8,128)(2,1)}), bf16[128,16,128]{0,2,1:T(8,128)(2,1)S(1)}, u32[]{:S(2)}, u32[]{:S(2)}) %all-to-all-start.3) | async-done | bytes 524320 | tf_op jit(solution)/shard_map/all_to_all | solution.py:187
  49.1 4.6 %all-to-all-start = ((bf16[128,16,128]{0,2,1:T(8,128)(2,1)}), bf16[128,16,128]{0,2,1:T(8,128)(2,1)S(1)}, u32[]{:S(2)}, u32[]{:S(2)}) async-start(bf16[128,16,128]{0,2,1:T(8,128)(2,1)} %multiply_convert_fusion.1), calls=%async_computation | async-start | bytes 1048576 | tf_op jit(solution)/shard_map/all_to_all | solution.py:185
  55.2 1.2 multiply_convert_fusion
  56.3 13.2 %all-to-all-done = bf16[128,16,128]{0,2,1:T(8,128)(2,1)S(1)} async-done(((bf16[128,16,128]{0,2,1:T(8,128)(2,1)}), bf16[128,16,128]{0,2,1:T(8,128)(2,1)S(1)}, u32[]{:S(2)}, u32[]{:S(2)}) %all-to-all-start) | async-done | bytes 524320 | tf_op jit(solution)/shard_map/all_to_all | solution.py:185
  69.5 4.4 %all-to-all-start.2 = ((bf16[128,16,128]{0,2,1:T(8,128)(2,1)}), bf16[128,16,128]{0,2,1:T(8,128)(2,1)S(1)}, u32[]{:S(2)}, u32[]{:S(2)}) async-start(bf16[128,16,128]{0,2,1:T(8,128)(2,1)} %multiply_convert_fusion), calls=%async_computation.2 | async-start | bytes 1048576 | tf_op jit(solution)/shard_map/all_to_all | solution.py:184
  74.6 30.5 %all_gather.3 = s32[1,2048]{1,0:T(1,128)S(1)} all-gather(s32[1,128]{1,0:T(1,128)S(1)} %copy-done.14), channel_id=1, replica_groups=mesh['dp'=16,'seq'=16] {'seq'}, dimensions={1}, use_global_device_ids=true | all-gather | bytes 8704 | tf_op jit(solution)/shard_map/all_gather | solution.py:190
  105.2 1.0 copy.60
  106.5 1.0 copy.58
  107.8 68.2 %while.123 = (s32[]{:T(128)}, f32[4,1,512]{2,1,0:T(1,128)S(1)}, f32[4,1,512]{2,1,0:T(1,128)S(1)}, s32[4]{0:T(128)S(1)}, bf16[2048,1,128]{2,0,1:T(8,128)(2,1)S(1)...) while((s32[]{:T(128)}, f32[4,1,512]{2,1,0:T(1,128)S(1)}, ...), condition=%wide.region_10.11_spmd.clone.clone, body=%wide.region_2.10_spmd.clone.clone.sunk | while | flops 474612736 | bytes 5606336 | solution.py:103
  110.6 7.0 %while.126 = (s32[]{:T(128)}, f32[1,512]{1,0:T(1,128)S(1)}, f32[1,512]{1,0:T(1,128)S(1)}, f32[512,1,128]{0,2,1:T(8,128)S(1)}, s32[]{:T(128)}, /*index=5*/s32[]{:...) while((s32[]{:T(128)}, f32[1,512]{1,0:T(1,128)S(1)}, ...), condition=%wide.region_8.8_spmd.clone, body=%wide.region_3.7_spmd.clone.sunk | while | flops 474350592 | bytes 4137481 | solution.py:97
  113.2 4.3 %conditional.7 = ((f32[1,512]{1,0:T(1,128)S(1)}, f32[1,512]{1,0:T(1,128)S(1)}, f32[512,1,128]{0,2,1:T(8,128)S(1)})) conditional(s32[]{:T(128)} %convert_element_type.212, (f32[1,512]{1,0:T(1,128)S(1)}, f32[1,512]{1,0:T(1,128)S(1)}, f32[512,1,128]{0,2,1:T(8,128)S(1)}) %tuple.208, (s32[]{:T(128)}, s32[2048]{0:T(1024)S(1)}, s32[]{:T(128)}, ...), branch_computations={%region_4.3_spmd, %region_5.6_spmd} | conditional | flops 474350592 | bytes 4137108 | solution.py:90
  114.1 1.3 fusion.62
  115.7 1.7 fusion.6
  120.4 13.9 %while.126 = (s32[]{:T(128)}, f32[1,512]{1,0:T(1,128)S(1)}, f32[1,512]{1,0:T(1,128)S(1)}, f32[512,1,128]{0,2,1:T(8,128)S(1)}, s32[]{:T(128)}, /*index=5*/s32[]{:...) while((s32[]{:T(128)}, f32[1,512]{1,0:T(1,128)S(1)}, ...), condition=%wide.region_8.8_spmd.clone, body=%wide.region_3.7_spmd.clone.sunk | while | flops 474350592 | bytes 4137481 | solution.py:97
  123.0 4.3 %conditional.7 = ((f32[1,512]{1,0:T(1,128)S(1)}, f32[1,512]{1,0:T(1,128)S(1)}, f32[512,1,128]{0,2,1:T(8,128)S(1)})) conditional(s32[]{:T(128)} %convert_element_type.212, (f32[1,512]{1,0:T(1,128)S(1)}, f32[1,512]{1,0:T(1,128)S(1)}, f32[512,1,128]{0,2,1:T(8,128)S(1)}) %tuple.208, (s32[]{:T(128)}, s32[2048]{0:T(1024)S(1)}, s32[]{:T(128)}, ...), branch_computations={%region_4.3_spmd, %region_5.6_spmd} | conditional | flops 474350592 | bytes 4137108 | solution.py:90
  123.9 1.3 fusion.62
  125.6 1.7 fusion.6
  130.0 4.3 %conditional.7 = ((f32[1,512]{1,0:T(1,128)S(1)}, f32[1,512]{1,0:T(1,128)S(1)}, f32[512,1,128]{0,2,1:T(8,128)S(1)})) conditional(s32[]{:T(128)} %convert_element_type.212, (f32[1,512]{1,0:T(1,128)S(1)}, f32[1,512]{1,0:T(1,128)S(1)}, f32[512,1,128]{0,2,1:T(8,128)S(1)}) %tuple.208, (s32[]{:T(128)}, s32[2048]{0:T(1024)S(1)}, s32[]{:T(128)}, ...), branch_computations={%region_4.3_spmd, %region_5.6_spmd} | conditional | flops 474350592 | bytes 4137108 | solution.py:90
  130.9 1.3 fusion.62
  132.5 1.7 fusion.6
  137.2 16.6 %while.126 = (s32[]{:T(128)}, f32[1,512]{1,0:T(1,128)S(1)}, f32[1,512]{1,0:T(1,128)S(1)}, f32[512,1,128]{0,2,1:T(8,128)S(1)}, s32[]{:T(128)}, /*index=5*/s32[]{:...) while((s32[]{:T(128)}, f32[1,512]{1,0:T(1,128)S(1)}, ...), condition=%wide.region_8.8_spmd.clone, body=%wide.region_3.7_spmd.clone.sunk | while | flops 474350592 | bytes 4137481 | solution.py:97
  142.5 4.3 %conditional.7 = ((f32[1,512]{1,0:T(1,128)S(1)}, f32[1,512]{1,0:T(1,128)S(1)}, f32[512,1,128]{0,2,1:T(8,128)S(1)})) conditional(s32[]{:T(128)} %convert_element_type.212, (f32[1,512]{1,0:T(1,128)S(1)}, f32[1,512]{1,0:T(1,128)S(1)}, f32[512,1,128]{0,2,1:T(8,128)S(1)}) %tuple.208, (s32[]{:T(128)}, s32[2048]{0:T(1024)S(1)}, s32[]{:T(128)}, ...), branch_computations={%region_4.3_spmd, %region_5.6_spmd} | conditional | flops 474350592 | bytes 4137108 | solution.py:90
  143.4 1.3 fusion.62
  145.0 1.7 fusion.6
  149.4 4.3 %conditional.7 = ((f32[1,512]{1,0:T(1,128)S(1)}, f32[1,512]{1,0:T(1,128)S(1)}, f32[512,1,128]{0,2,1:T(8,128)S(1)})) conditional(s32[]{:T(128)} %convert_element_type.212, (f32[1,512]{1,0:T(1,128)S(1)}, f32[1,512]{1,0:T(1,128)S(1)}, f32[512,1,128]{0,2,1:T(8,128)S(1)}) %tuple.208, (s32[]{:T(128)}, s32[2048]{0:T(1024)S(1)}, s32[]{:T(128)}, ...), branch_computations={%region_4.3_spmd, %region_5.6_spmd} | conditional | flops 474350592 | bytes 4137108 | solution.py:90
  150.3 1.3 fusion.62
  152.0 1.7 fusion.6
  156.6 19.2 %while.126 = (s32[]{:T(128)}, f32[1,512]{1,0:T(1,128)S(1)}, f32[1,512]{1,0:T(1,128)S(1)}, f32[512,1,128]{0,2,1:T(8,128)S(1)}, s32[]{:T(128)}, /*index=5*/s32[]{:...) while((s32[]{:T(128)}, f32[1,512]{1,0:T(1,128)S(1)}, ...), condition=%wide.region_8.8_spmd.clone, body=%wide.region_3.7_spmd.clone.sunk | while | flops 474350592 | bytes 4137481 | solution.py:97
  164.6 4.3 %conditional.7 = ((f32[1,512]{1,0:T(1,128)S(1)}, f32[1,512]{1,0:T(1,128)S(1)}, f32[512,1,128]{0,2,1:T(8,128)S(1)})) conditional(s32[]{:T(128)} %convert_element_type.212, (f32[1,512]{1,0:T(1,128)S(1)}, f32[1,512]{1,0:T(1,128)S(1)}, f32[512,1,128]{0,2,1:T(8,128)S(1)}) %tuple.208, (s32[]{:T(128)}, s32[2048]{0:T(1024)S(1)}, s32[]{:T(128)}, ...), branch_computations={%region_4.3_spmd, %region_5.6_spmd} | conditional | flops 474350592 | bytes 4137108 | solution.py:90
  165.5 1.3 fusion.62
  167.1 1.7 fusion.6
  171.5 4.3 %conditional.7 = ((f32[1,512]{1,0:T(1,128)S(1)}, f32[1,512]{1,0:T(1,128)S(1)}, f32[512,1,128]{0,2,1:T(8,128)S(1)})) conditional(s32[]{:T(128)} %convert_element_type.212, (f32[1,512]{1,0:T(1,128)S(1)}, f32[1,512]{1,0:T(1,128)S(1)}, f32[512,1,128]{0,2,1:T(8,128)S(1)}) %tuple.208, (s32[]{:T(128)}, s32[2048]{0:T(1024)S(1)}, s32[]{:T(128)}, ...), branch_computations={%region_4.3_spmd, %region_5.6_spmd} | conditional | flops 474350592 | bytes 4137108 | solution.py:90
  172.4 1.3 fusion.62
  174.1 1.7 fusion.6
  176.0 64.2 %while.125 = (s32[]{:T(128)}, f32[2048,1,128]{2,0,1:T(8,128)S(1)}, bf16[4,512,1,128]{3,1,0,2:T(8,128)(2,1)}, bf16[4,512,1,128]{3,1,0,2:T(8,128)(2,1)}, s32[4]{0:...) while((s32[]{:T(128)}, f32[2048,1,128]{2,0,1:T(8,128)S(1)}, ...), condition=%wide.region_16.17_spmd.clone.clone, body=%wide.region_11.16_spmd.clone.clone.sunk | while | flops 338690048 | bytes 9876548 | solution.py:152
  180.4 15.0 %while.127 = (s32[]{:T(128)}, f32[2048,1,128]{2,0,1:T(8,128)S(1)}, f32[512,1,128]{0,2,1:T(8,128)S(1)}, f32[512,1,128]{0,2,1:T(8,128)S(1)}, s32[]{:T(128)}, /*ind...) while((s32[]{:T(128)}, f32[2048,1,128]{2,0,1:T(8,128)S(1)}, ...), condition=%wide.region_15.15_spmd.clone, body=%wide.region_12.14_spmd.clone.sunk | while | flops 338624512 | bytes 7246415 | solution.py:149
  182.9 2.5 conditional.6
  187.9 2.5 conditional.6
  200.8 12.5 %while.127 = (s32[]{:T(128)}, f32[2048,1,128]{2,0,1:T(8,128)S(1)}, f32[512,1,128]{0,2,1:T(8,128)S(1)}, f32[512,1,128]{0,2,1:T(8,128)S(1)}, s32[]{:T(128)}, /*ind...) while((s32[]{:T(128)}, f32[2048,1,128]{2,0,1:T(8,128)S(1)}, ...), condition=%wide.region_15.15_spmd.clone, body=%wide.region_12.14_spmd.clone.sunk | while | flops 338624512 | bytes 7246415 | solution.py:149
  203.3 2.5 conditional.6
  208.3 2.5 conditional.6
  218.8 10.0 %while.127 = (s32[]{:T(128)}, f32[2048,1,128]{2,0,1:T(8,128)S(1)}, f32[512,1,128]{0,2,1:T(8,128)S(1)}, f32[512,1,128]{0,2,1:T(8,128)S(1)}, s32[]{:T(128)}, /*ind...) while((s32[]{:T(128)}, f32[2048,1,128]{2,0,1:T(8,128)S(1)}, ...), condition=%wide.region_15.15_spmd.clone, body=%wide.region_12.14_spmd.clone.sunk | while | flops 338624512 | bytes 7246415 | solution.py:149
  221.2 2.5 conditional.6
  226.2 2.5 conditional.6
  234.2 5.0 %while.127 = (s32[]{:T(128)}, f32[2048,1,128]{2,0,1:T(8,128)S(1)}, f32[512,1,128]{0,2,1:T(8,128)S(1)}, f32[512,1,128]{0,2,1:T(8,128)S(1)}, s32[]{:T(128)}, /*ind...) while((s32[]{:T(128)}, f32[2048,1,128]{2,0,1:T(8,128)S(1)}, ...), condition=%wide.region_15.15_spmd.clone, body=%wide.region_12.14_spmd.clone.sunk | while | flops 338624512 | bytes 7246415 | solution.py:149
  236.7 2.5 conditional.6
  240.8 2.1 reduce.13
  243.7 8.2 %all-to-all-start.6 = ((bf16[16,2,8192]{2,1,0:T(2,128)(2,1)}), bf16[16,2,8192]{2,1,0:T(2,128)(2,1)S(1)}, u32[]{:S(2)}, u32[]{:S(2)}) async-start(bf16[16,2,8192]{2,1,0:T(2,128)(2,1)} %reshape.278), calls=%async_computation.6 | async-start | bytes 1048576 | tf_op jit(solution)/shard_map/all_to_all | solution.py:200
  252.0 1.0 reduce.12
  253.9 9.9 %all-to-all-done.6 = bf16[16,2,8192]{2,1,0:T(2,128)(2,1)S(1)} async-done(((bf16[16,2,8192]{2,1,0:T(2,128)(2,1)}), bf16[16,2,8192]{2,1,0:T(2,128)(2,1)S(1)}, u32[]{:S(2)}, u32[]{:S(2)}) %all-to-all-start.6) | async-done | bytes 524320 | tf_op jit(solution)/shard_map/all_to_all | solution.py:200
  263.8 3.6 all-to-all-start.5
  267.5 1.0 reduce.11
  269.4 10.5 %all-to-all-done.5 = bf16[16,2,8192]{2,1,0:T(2,128)(2,1)S(1)} async-done(((bf16[16,2,8192]{2,1,0:T(2,128)(2,1)}), bf16[16,2,8192]{2,1,0:T(2,128)(2,1)S(1)}, u32[]{:S(2)}, u32[]{:S(2)}) %all-to-all-start.5) | async-done | bytes 524320 | tf_op jit(solution)/shard_map/all_to_all | solution.py:196
  280.7 4.4 %all-to-all-start.4 = ((bf16[16,2,8192]{2,1,0:T(2,128)(2,1)}), bf16[16,2,8192]{2,1,0:T(2,128)(2,1)}, u32[]{:S(2)}, u32[]{:S(2)}) async-start(bf16[16,2,8192]{2,1,0:T(2,128)(2,1)} %reshape.274), calls=%async_computation.4 | async-start | bytes 1048576 | tf_op jit(solution)/shard_map/all_to_all | solution.py:193
  286.1 1.0 copy.77
  290.4 1.0 copy.76
  291.4 5.5 %all-to-all-done.4 = bf16[16,2,8192]{2,1,0:T(2,128)(2,1)} async-done(((bf16[16,2,8192]{2,1,0:T(2,128)(2,1)}), bf16[16,2,8192]{2,1,0:T(2,128)(2,1)}, u32[]{:S(2)}, u32[]{:S(2)}) %all-to-all-start.4) | async-done | bytes 524320 | tf_op jit(solution)/shard_map/all_to_all | solution.py:193
  296.9 2.2 reshape.275
  301.1 87.1 %all-reduce = (f32[2048]{0:T(1024)S(1)}, f32[2048]{0:T(1024)S(1)}) all-reduce(f32[2048]{0:T(1024)S(1)} %bitcast.225, f32[2048]{0:T(1024)S(1)} %bitcast.224), channel_id=1, replica_groups=mesh['dp'=16,'seq'=16] {'dp','seq'}, use_global_device_ids=true, to_apply=%region_20.21 | all-reduce | flops 4096 | bytes 32768 | tf_op jit(solution)/shard_map/psum | solution.py:203
  (295 shorter events, 70.2 us)
Async XLA Ops:
  2.7 10.2 %copy-start.8 = (bf16[1,128,2048]{2,1,0:T(8,128)(2,1)S(1)}, bf16[1,128,2048]{2,1,0:T(8,128)(2,1)}, u32[]{:S(2)}) copy-start(bf16[1,128,2048]{2,1,0:T(8,128)(2,1)} %param.22) | copy-start | bytes 1572868
  2.7 25.8 %all-to-all-start.1 = ((bf16[128,16,128]{0,2,1:T(8,128)(2,1)}), bf16[128,16,128]{0,2,1:T(8,128)(2,1)S(1)}, u32[]{:S(2)}, u32[]{:S(2)}) async-start(bf16[128,16,128]{0,2,1:T(8,128)(2,1)} %bitcast.30), calls=%async_computation.1 | async-start | bytes 1048576 | tf_op jit(solution)/shard_map/all_to_all | solution.py:186
  28.5 4.9 %copy-start.9 = (bf16[1,128,2048]{2,1,0:T(8,128)(2,1)S(1)}, bf16[1,128,2048]{2,1,0:T(8,128)(2,1)}, u32[]{:S(2)}) copy-start(bf16[1,128,2048]{2,1,0:T(8,128)(2,1)} %param.20) | copy-start | bytes 1572868
  28.5 20.6 %all-to-all-start.3 = ((bf16[128,16,128]{0,2,1:T(8,128)(2,1)}), bf16[128,16,128]{0,2,1:T(8,128)(2,1)S(1)}, u32[]{:S(2)}, u32[]{:S(2)}) async-start(bf16[128,16,128]{0,2,1:T(8,128)(2,1)} %bitcast.39), calls=%async_computation.3 | async-start | bytes 1048576 | tf_op jit(solution)/shard_map/all_to_all | solution.py:187
  33.7 0.8 copy-start.4
  34.5 1.0 copy-start.2
  34.5 1.0 copy-start.12
  36.7 17.1 %copy-start.10 = (bf16[1,128,2048]{2,1,0:T(8,128)(2,1)S(1)}, bf16[1,128,2048]{2,1,0:T(8,128)(2,1)}, u32[]{:S(2)}) copy-start(bf16[1,128,2048]{2,1,0:T(8,128)(2,1)} %param.19) | copy-start | bytes 1572868
  49.1 20.4 %all-to-all-start = ((bf16[128,16,128]{0,2,1:T(8,128)(2,1)}), bf16[128,16,128]{0,2,1:T(8,128)(2,1)S(1)}, u32[]{:S(2)}, u32[]{:S(2)}) async-start(bf16[128,16,128]{0,2,1:T(8,128)(2,1)} %multiply_convert_fusion.1), calls=%async_computation | async-start | bytes 1048576 | tf_op jit(solution)/shard_map/all_to_all | solution.py:185
  54.2 1.0 copy-start
  54.2 1.0 copy-start.13
  69.5 38.0 %all-to-all-start.2 = ((bf16[128,16,128]{0,2,1:T(8,128)(2,1)}), bf16[128,16,128]{0,2,1:T(8,128)(2,1)S(1)}, u32[]{:S(2)}, u32[]{:S(2)}) async-start(bf16[128,16,128]{0,2,1:T(8,128)(2,1)} %multiply_convert_fusion), calls=%async_computation.2 | async-start | bytes 1048576 | tf_op jit(solution)/shard_map/all_to_all | solution.py:184
  74.0 0.7 copy-start.14
  243.7 8.2 %copy-start.11 = (bf16[4,512,1,128]{3,1,0,2:T(8,128)(2,1)S(1)}, bf16[4,512,1,128]{3,1,0,2:T(8,128)(2,1)}, u32[]{:S(2)}) copy-start(bf16[4,512,1,128]{3,1,0,2:T(8,128)(2,1)} %get-tuple-element.1079) | copy-start | bytes 1572868
  243.7 20.1 %all-to-all-start.6 = ((bf16[16,2,8192]{2,1,0:T(2,128)(2,1)}), bf16[16,2,8192]{2,1,0:T(2,128)(2,1)S(1)}, u32[]{:S(2)}, u32[]{:S(2)}) async-start(bf16[16,2,8192]{2,1,0:T(2,128)(2,1)} %reshape.278), calls=%async_computation.6 | async-start | bytes 1048576 | tf_op jit(solution)/shard_map/all_to_all | solution.py:200
  263.8 16.1 %all-to-all-start.5 = ((bf16[16,2,8192]{2,1,0:T(2,128)(2,1)}), bf16[16,2,8192]{2,1,0:T(2,128)(2,1)S(1)}, u32[]{:S(2)}, u32[]{:S(2)}) async-start(bf16[16,2,8192]{2,1,0:T(2,128)(2,1)} %reshape.276), calls=%async_computation.5 | async-start | bytes 1048576 | tf_op jit(solution)/shard_map/all_to_all | solution.py:196
  280.0 0.8 copy-start.6
  280.7 16.1 %all-to-all-start.4 = ((bf16[16,2,8192]{2,1,0:T(2,128)(2,1)}), bf16[16,2,8192]{2,1,0:T(2,128)(2,1)}, u32[]{:S(2)}, u32[]{:S(2)}) async-start(bf16[16,2,8192]{2,1,0:T(2,128)(2,1)} %reshape.274), calls=%async_computation.4 | async-start | bytes 1048576 | tf_op jit(solution)/shard_map/all_to_all | solution.py:193
  286.1 1.0 copy-start.7
  287.8 1.2 copy-start.3
  289.0 1.0 copy-start.5
  299.2 1.2 copy-start.1
where the time goes:
time: 393 us; the launch traced here: 391 us
  blocking collectives  118 us (30%)
  waiting for transfers between devices  66.2 us (17%)
  local copies, waits for them, and re-layouts  61.9 us (16%)
  loops' own time  59.6 us (15%)
  starting transfers between devices  40.4 us (10%)
  matrix products  32.3 us (8%)
  other arithmetic  11.8 us (3%)
    psum x1, blocking collectives, body(): lax.psum((q_terms.reshape(feature), k_terms.reshape(feature)), ('dp', 'se...  87.1 us
    all_gather x1, blocking collectives, body(): segs = lax.all_gather(doc_ids, 'seq', axis=1, tiled=True)[0]  30.5 us
    another operation x4, loops' own time, row_stats(): lax.fori_loop(0, query_idx + 1, row_guarded, start)  19.9 us
    unnamed x44, local copies, waits for them, and re-layouts  19.1 us
    another operation x4, loops' own time, key_block(): dq_all, dk_acc, dv_acc = lax.fori_loop(key_idx, nblocks, key_guarded, start)  18.9 us
    all_to_all x1, waiting for transfers between devices, body(): lax.all_to_all(packed_v, 'seq', split_axis=1, concat_axis=0, tiled=True)  14.6 us
    all_to_all x1, waiting for transfers between devices, body(): lax.all_to_all(packed_k, 'seq', split_axis=1, concat_axis=0, tiled=True)  13.2 us
    all_to_all x1, waiting for transfers between devices, body(): lax.all_to_all(packed_d, 'seq', split_axis=1, concat_axis=0, tiled=True)  12.5 us
  transfers between devices with their start and end apart: 7, of which 6 were waited for; matrix products, arithmetic and copies ran while one was open for 4% of the time, Pallas kernels for 0%

commit v1 on v0

v1 whole, which is shorter than its diff:
```python
import functools

import jax
import jax.numpy as jnp
from jax import lax
from jax.experimental import pallas as pl
from jax.experimental.pallas import tpu as pltpu
from jax.sharding import PartitionSpec as P

HD = 128
EPS = 1e-06
MASKED = -1e30
LOG2E = 1.4426950408889634
SCALE = HD ** (-0.5)

BLOCK = 128
REACH = 4
SLOTS = REACH + 1
GROUP = 1
FORWARD, ACROSS, QUERIES, KEYS = 1, 2, 3, 4


def dot_nt(a, b):
    return lax.dot_general(a, b, (((1,), (1,)), ((), ())), preferred_element_type=jnp.float32)


def dot_nn(a, b):
    return lax.dot_general(a, b, (((1,), (0,)), ((), ())), preferred_element_type=jnp.float32)


def inverse_rms(x):
    return lax.rsqrt(jnp.mean(x * x, axis=-1, keepdims=True) + EPS)


def kernel(
    n_seq, n_dp, heads,
    q_ref, k_ref, v_ref, d_ref, doc_ref, gq_ref, gk_ref,
    dq_out, dk_out, dv_out, gq_out, gk_out,
    kvw, qdw, docw, statw, bias_q, bias_k, gsend, grecv, tsend, trecv,
    kv_s, kv_r, qd_s, qd_r, doc_s, doc_r, stat_s, stat_r, gain_s, gain_r, tot_s, tot_r,
):
    me = lax.axis_index("seq")
    row = lax.axis_index("dp")
    side = lax.rem(me, 2)
    partner = me + 1 - 2 * side
    up = lax.rem(me + 2, n_seq)
    down = lax.rem(me + n_seq - 2, n_seq)
    chunks = heads // GROUP

    def remote(src, dst, send, recv, device):
        return pltpu.make_async_remote_copy(
            src_ref=src, dst_ref=dst, send_sem=send, recv_sem=recv,
            device_id=device, device_id_type=pl.DeviceIdType.MESH,
        )

    def kv(c, src, dst, target):
        return remote(kvw.at[c, src], kvw.at[c, dst], kv_s.at[c, dst], kv_r.at[c, dst], {"seq": target})

    def qd(c, src, dst, target):
        return remote(qdw.at[c, src], qdw.at[c, dst], qd_s.at[c, dst], qd_r.at[c, dst], {"seq": target})

    def doc(o):
        target = lax.rem(me + o + n_seq, n_seq)
        s = REACH - o
        return remote(docw.at[REACH], docw.at[s], doc_s.at[s], doc_r.at[s], {"seq": target})

    def stat(c, t):
        target = lax.rem(me - t + n_seq, n_seq)
        return remote(statw.at[c, 0], statw.at[c, t], stat_s.at[c, t], stat_r.at[c, t], {"seq": target})

    def gain(h, source):
        return remote(gsend.at[h], grecv.at[source], gain_s.at[h], gain_r.at[source], {"seq": h})

    def total(p, source):
        return remote(tsend, trecv.at[source], tot_s.at[p], tot_r.at[source], {"dp": p})

    offsets = [o for o in range(-REACH, REACH + 1) if o != 0]

    barrier = pltpu.get_barrier_semaphore()

    def greet_seq(p, carry):
        @pl.when(p != me)
        def _():
            pl.semaphore_signal(barrier, inc=1, device_id={"seq": p}, device_id_type=pl.DeviceIdType.MESH)
        return carry

    def greet_dp(p, carry):
        @pl.when(p != row)
        def _():
            pl.semaphore_signal(barrier, inc=1, device_id={"dp": p}, device_id_type=pl.DeviceIdType.MESH)
        return carry

    lax.fori_loop(0, n_seq, greet_seq, 0)
    lax.fori_loop(0, n_dp, greet_dp, 0)
    docw[REACH] = jnp.broadcast_to(doc_ref[...].astype(jnp.float32), (8, BLOCK))
    pl.semaphore_wait(barrier, n_seq - 1 + n_dp - 1)
    for o in offsets:
        doc(o).start()

    def lanes(h):
        return pl.ds(pl.multiple_of(h * HD, HD), HD)

    def normed(ref, gains, h):
        x = ref[:, lanes(h)].astype(jnp.float32)
        return (x * inverse_rms(x) * gains[pl.ds(h, 1), :]).astype(jnp.bfloat16)

    def first(c):
        for g in range(GROUP):
            h = c * GROUP + g
            kvw[c, REACH, g, 0] = normed(k_ref, gk_ref, h)
            kvw[c, REACH, g, 1] = v_ref[:, lanes(h)]
            qdw[c, 0, g, 0] = normed(q_ref, gq_ref, h)
            qdw[c, 0, g, 1] = d_ref[:, lanes(h)]
        kv(c, 4, 2, up).start()
        qd(c, 0, 2, down).start()

        @pl.when(side == 0)
        def _():
            kv(c, 4, 3, partner).start()

        @pl.when(side == 1)
        def _():
            qd(c, 0, 1, partner).start()

    def forward(c):
        kv(c, 4, 2, up).wait_recv()
        kv(c, 2, 0, up).start()
        kv(c, 2, 1 + 2 * side, partner).start()
        qd(c, 0, 2, down).wait_recv()
        qd(c, 2, 4, down).start()
        qd(c, 2, 1 + 2 * side, partner).start()

    def across(c):
        kv(c, 2, 0, up).wait_recv()
        qd(c, 2, 4, down).wait_recv()

        @pl.when(side == 1)
        def _():
            kv(c, 0, 1, partner).start()

        @pl.when(side == 0)
        def _():
            qd(c, 4, 3, partner).start()

    def masks():
        for o in offsets:
            doc(o).wait_recv()
        own = jnp.broadcast_to(docw[REACH, 0:1, :], (BLOCK, BLOCK)).T
        rows = lax.broadcasted_iota(jnp.int32, (BLOCK, BLOCK), 0)
        cols = lax.broadcasted_iota(jnp.int32, (BLOCK, BLOCK), 1)
        for s in range(SLOTS):
            ids = jnp.where(me - REACH + s >= 0, docw[s, 0:1, :], -1.0)
            allowed = own == ids
            if s == REACH:
                allowed = allowed & (cols <= rows)
            bias_q[:, s * BLOCK:(s + 1) * BLOCK] = jnp.where(allowed, 0.0, MASKED)
        for t in range(SLOTS):
            ids = jnp.where(me + t < n_seq, docw[REACH + t, 0:1, :], -1.0)
            allowed = own == ids
            if t == 0:
                allowed = allowed & (rows <= cols)
            bias_k[:, t * BLOCK:(t + 1) * BLOCK] = jnp.where(allowed, 0.0, MASKED)

    def norm_back(ref, gains, h, grad):
        x = ref[:, lanes(h)].astype(jnp.float32)
        rec = inverse_rms(x)
        hat = x * rec
        scaled = grad * gains[pl.ds(h, 1), :]
        back = rec * (scaled - hat * jnp.mean(scaled * hat, axis=-1, keepdims=True))
        return back.astype(jnp.bfloat16), jnp.sum(grad * hat, axis=0, keepdims=True)

    def window(ref, c, g, i):
        return ref[c, :, g, i].reshape(SLOTS * BLOCK, HD)

    def queries(c):
        kv(c, 4, 3, partner).wait_recv()
        kv(c, 4, 1, partner).wait_recv()
        lane = lax.broadcasted_iota(jnp.int32, (BLOCK, BLOCK), 1)
        stats = jnp.zeros((BLOCK, BLOCK), jnp.float32)
        for g in range(GROUP):
            h = c * GROUP + g
            keys = window(kvw, c, g, 0)
            s = dot_nt(qdw[c, 0, g, 0], keys) * (SCALE * LOG2E) + bias_q[...]
            dprob = dot_nt(qdw[c, 0, g, 1], window(kvw, c, g, 1))
            peak = jnp.max(s, axis=1, keepdims=True)
            e = jnp.exp2(s - peak)
            weight = jnp.sum(e, axis=1, keepdims=True)
            inv = 1.0 / weight
            delta = jnp.sum(e * dprob, axis=1, keepdims=True) * inv
            dscore = (e * (inv * SCALE) * (dprob - delta)).astype(jnp.bfloat16)
            grad, term = norm_back(q_ref, gq_ref, h, dot_nn(dscore, keys))
            dq_out[:, lanes(h)] = grad
            gsend[h] = jnp.broadcast_to(term, (8, HD))
            stats = jnp.where(lane == 2 * g, peak + jnp.log2(weight), stats)
            stats = jnp.where(lane == 2 * g + 1, delta, stats)
        statw[c, 0] = stats.T[0:8]
        for t in range(1, SLOTS):
            stat(c, t).start()

    def keys_side(c):
        qd(c, 0, 1, partner).wait_recv()
        qd(c, 0, 3, partner).wait_recv()
        for t in range(1, SLOTS):
            stat(c, t).wait_recv()
        for g in range(GROUP):
            h = c * GROUP + g
            lse = jnp.concatenate([statw[c, t, 2 * g:2 * g + 1, :] for t in range(SLOTS)], axis=1)
            delta = jnp.concatenate([statw[c, t, 2 * g + 1:2 * g + 2, :] for t in range(SLOTS)], axis=1)
            qs = window(qdw, c, g, 0)
            ds = window(qdw, c, g, 1)
            s = dot_nt(kvw[c, REACH, g, 0], qs) * (SCALE * LOG2E) + bias_k[...]
            p = jnp.exp2(s - lse)
            dv_out[:, lanes(h)] = dot_nn(p.astype(jnp.bfloat16), ds).astype(jnp.bfloat16)
            dprob = dot_nt(kvw[c, REACH, g, 1], ds)
            dscore = (p * SCALE * (dprob - delta)).astype(jnp.bfloat16)
            grad, term = norm_back(k_ref, gk_ref, h, dot_nn(dscore, qs))
            dk_out[:, lanes(h)] = grad
            gsend[h, 1:2] = term

            @pl.when(h != me)
            def _():
                gain(h, me).start()

    def step(t, carry):
        @pl.when(t < chunks)
        def _():
            first(t)

        @pl.when((t >= FORWARD) & (t < chunks + FORWARD))
        def _():
            forward(t - FORWARD)

        @pl.when((t >= ACROSS) & (t < chunks + ACROSS))
        def _():
            across(t - ACROSS)

        @pl.when(t == QUERIES)
        def _():
            masks()

        @pl.when((t >= QUERIES) & (t < chunks + QUERIES))
        def _():
            queries(t - QUERIES)

        @pl.when((t >= KEYS) & (t < chunks + KEYS))
        def _():
            keys_side(t - KEYS)

        return carry

    lax.fori_loop(0, chunks + KEYS, step, 0)

    grecv[me] = gsend[me]

    def gain_wait(p, carry):
        @pl.when(p != me)
        def _():
            gain(me, p).wait_recv()
        return carry

    lax.fori_loop(0, n_seq, gain_wait, 0)
    tsend[...] = jnp.sum(grecv[...], axis=0)
    trecv[row] = tsend[...]

    def total_send(p, carry):
        @pl.when(p != row)
        def _():
            total(p, row).start()
        return carry

    lax.fori_loop(0, n_dp, total_send, 0)

    def drain(c, carry):
        for slot in range(REACH):
            kv(c, 4, slot, partner).wait_send()
            qd(c, 0, slot + 1, partner).wait_send()
            stat(c, slot + 1).wait_send()
        return carry

    lax.fori_loop(0, chunks, drain, 0)
    for o in offsets:
        doc(o).wait_send()

    def gain_drain(p, carry):
        @pl.when(p != me)
        def _():
            gain(p, me).wait_send()
        return carry

    lax.fori_loop(0, n_seq, gain_drain, 0)

    def total_wait(p, carry):
        @pl.when(p != row)
        def _():
            total(p, p).wait_recv()
            total(p, p).wait_send()
        return carry

    lax.fori_loop(0, n_dp, total_wait, 0)
    sums = jnp.sum(trecv[...], axis=0)
    gq_out[...] = sums[0:1]
    gk_out[...] = sums[1:2]


def body(query_states, key_states, value_states, out_grad, doc_ids, query_gain, key_gain):
    n_seq = lax.axis_size("seq")
    n_dp = lax.axis_size("dp")
    rows, feature = query_states.shape[1:]
    heads = feature // HD
    chunks = heads // GROUP
    window = (chunks, SLOTS, GROUP, 2, BLOCK, HD)
    dma = pltpu.SemaphoreType.DMA
    vmem = pl.BlockSpec(memory_space=pltpu.VMEM)
    grad = jax.ShapeDtypeStruct((rows, feature), jnp.bfloat16)
    gain = jax.ShapeDtypeStruct((1, HD), jnp.float32)
    pairs = heads * rows * SLOTS * BLOCK
    outs = pl.pallas_call(
        functools.partial(kernel, n_seq, n_dp, heads),
        out_shape=(grad, grad, grad, gain, gain),
        in_specs=[vmem] * 7,
        out_specs=(vmem,) * 5,
        scratch_shapes=[
            pltpu.VMEM(window, jnp.bfloat16),
            pltpu.VMEM(window, jnp.bfloat16),
            pltpu.VMEM((2 * REACH + 1, 8, BLOCK), jnp.float32),
            pltpu.VMEM((chunks, SLOTS, 8, BLOCK), jnp.float32),
            pltpu.VMEM((BLOCK, SLOTS * BLOCK), jnp.float32),
            pltpu.VMEM((BLOCK, SLOTS * BLOCK), jnp.float32),
            pltpu.VMEM((heads, 8, HD), jnp.float32),
            pltpu.VMEM((n_seq, 8, HD), jnp.float32),
            pltpu.VMEM((8, HD), jnp.float32),
            pltpu.VMEM((n_dp, 8, HD), jnp.float32),
            dma((chunks, SLOTS)), dma((chunks, SLOTS)),
            dma((chunks, SLOTS)), dma((chunks, SLOTS)),
            dma((2 * REACH + 1,)), dma((2 * REACH + 1,)),
            dma((chunks, SLOTS)), dma((chunks, SLOTS)),
            dma((heads,)), dma((n_seq,)),
            dma((n_dp,)), dma((n_dp,)),
        ],
        cost_estimate=pl.CostEstimate(
            flops=14 * pairs * HD, bytes_accessed=7 * rows * feature * 2, transcendentals=2 * pairs
        ),
        compiler_params=pltpu.CompilerParams(
            collective_id=0, has_side_effects=True, vmem_limit_bytes=40 * 1024 * 1024
        ),
    )(
        query_states[0], key_states[0], value_states[0], out_grad[0], doc_ids,
        query_gain.reshape(heads, HD), key_gain.reshape(heads, HD),
    )
    dq, dk, dv, gq, gk = outs
    return (dq[None], dk[None], dv[None], gq[0], gk[0])


def solution(mesh):
    split = P("dp", "seq", None)
    return jax.shard_map(
        body,
        mesh=mesh,
        in_specs=(split, split, split, split, P("dp", "seq"), P(), P()),
        out_specs=(split, split, split, P("seq"), P("seq")),
        check_vma=False,
    )
```

time: 393 us -> 133 us (0.34)
  Pallas kernels: 0 us -> 123 us
  blocking collectives: 118 us -> 0 us
  waiting for transfers between devices: 66.2 us -> 0 us
  loops' own time: 59.6 us -> 0 us
  local copies, waits for them, and re-layouts: 61.9 us -> 8.95 us
  starting transfers between devices: 40.4 us -> 0 us
  matrix products: 32.3 us -> 0 us
  other arithmetic: 11.8 us -> 0 us
    pallas_call x0 -> x1, Pallas kernels: none -> 123 us  [body(): pl.pallas_call(functools.partial(kernel, n_seq, n_dp, heads), out_shape=(...]
    psum x1 -> x0, blocking collectives: 87.1 us -> none  [body(): lax.psum((q_terms.reshape(feature), k_terms.reshape(feature)), ('dp', 'se...]
    all_to_all x7 -> x0, waiting for transfers between devices: 66.2 us -> none  [the longest x1 14.6 us: body(): lax.all_to_all(packed_v, 'seq', split_axis=1, concat_axis=0, tiled=True)]
    another operation x30 -> x0, loops' own time: 59.6 us -> none  [the longest x4 19.9 us: row_stats(): lax.fori_loop(0, query_idx + 1, row_guarded, start)]
    all_to_all x7 -> x0, starting transfers between devices: 40.4 us -> none  [the longest x1 10.2 us: body(): lax.all_to_all(packed_v, 'seq', split_axis=1, concat_axis=0, tiled=True)]
    dynamic_slice x107 -> x0, local copies, waits for them, and re-layouts: 34.7 us -> none  [the longest x62 11.1 us: block_rows(): return lax.dynamic_slice_in_dim(array, index * block, block, 0)]
    dot_general x49 -> x0, matrix products: 32.3 us -> none  [the longest x7 12.1 us: add_key(): jnp.einsum('hqk,khd->qhd', prob, v_block, precision=lax.Precision.HIGHEST)]
    all_gather x1 -> x0, blocking collectives: 30.5 us -> none  [body(): segs = lax.all_gather(doc_ids, 'seq', axis=1, tiled=True)[0]]
  transfers between devices with their start and end apart: 7 -> 0, of which waited for: 6 -> 0; matrix products, arithmetic and copies ran while one was open for 4% -> 0% of each run, Pallas kernels for 0% -> 0%
where the time goes in v1:
time: 133 us; the launch traced here: 132 us
  Pallas kernels  123 us (92%)
  local copies, waits for them, and re-layouts  8.95 us (7%)
    pallas_call x1, Pallas kernels, body(): pl.pallas_call(functools.partial(kernel, n_seq, n_dp, heads), out_shape=(...  123 us
    unnamed x19, local copies, waits for them, and re-layouts  8.95 us

profile of v1, /device:TPU:1, one launch (start us, length us, event | category | flops | bytes accessed | tf_op | source)
XLA Modules:
  0.0 132.4 jit_solution(13165920475331449055)
XLA Ops:
  0.6 0.0 copy-start.4
  0.6 0.0 copy-start.6
  0.7 0.7 copy-done.4
  1.3 0.0 copy-done.6
  1.3 0.0 copy-start
  1.3 1.0 copy-done
  2.4 0.0 copy-start.1
  2.4 1.0 copy-done.1
  3.4 0.0 copy-start.2
  3.4 1.0 copy-done.2
  4.5 0.0 copy-start.3
  4.5 1.0 copy-done.3
  5.5 0.0 copy-start.5
  5.5 0.7 copy-done.5
  6.2 122.8 %shard_map.110 = (bf16[128,2048]{1,0:T(8,128)(2,1)S(1)}, bf16[128,2048]{1,0:T(8,128)(2,1)S(1)}, bf16[128,2048]{1,0:T(8,128)(2,1)S(1)}, f32[1,128]{1,0:T(1,128)S(1)}, f32[1,128]{1,0:T(1,128)S(1)}) custom-call(bf16[128,2048]{1,0:T(8,128)(2,1)S(1)} %bitcast.14, bf16[128,2048]{1,0:T(8,128)(2,1)S(1)} %bitcast.15, bf16[128,2048]{1,0:T(8,128)(2,1)S(1)} %bitcast.16, ...), custom_call_target="tpu_custom_call" | custom-call | flops 2348810240 | bytes 3670016 | tf_op jit(solution)/shard_map/pallas_call | solution.py:317
  129.0 0.8 copy.17
  129.8 0.8 copy.18
  130.6 0.8 copy.19
  131.4 0.5 copy.20
  131.9 0.5 copy.21
Async XLA Ops:
  0.6 0.7 copy-start.4
  0.6 0.7 copy-start.6
  1.3 1.0 copy-start
  2.4 1.0 copy-start.1
  3.4 1.0 copy-start.2
  4.5 1.0 copy-start.3
  5.5 0.7 copy-start.5

commit v2 on v1

v2 whole, which is shorter than its diff:
```python
import functools

import jax
import jax.numpy as jnp
from jax import lax
from jax.experimental import pallas as pl
from jax.experimental.pallas import tpu as pltpu
from jax.sharding import PartitionSpec as P

HD = 128
EPS = 1e-06
MASKED = -1e30
LOG2E = 1.4426950408889634
SCALE = HD ** (-0.5)

BLOCK = 128
PAIR = 2 * BLOCK
REACH = 2
SLOTS = REACH + 1
SPAN = 5 * BLOCK
MESH = pl.DeviceIdType.MESH
AHEAD, FORWARD, QUERIES, KEYS = 2, 1, 2, 3


def dot_nt(a, b):
    return lax.dot_general(a, b, (((1,), (1,)), ((), ())), preferred_element_type=jnp.float32)


def dot_nn(a, b):
    return lax.dot_general(a, b, (((1,), (0,)), ((), ())), preferred_element_type=jnp.float32)


def inverse_rms(x):
    return lax.rsqrt(jnp.mean(x * x, axis=-1, keepdims=True) + EPS)


def kernel(
    n_seq, n_dp, heads,
    q_ref, k_ref, v_ref, d_ref, doc_ref, gq_ref, gk_ref,
    dq_out, dk_out, dv_out, gq_out, gk_out,
    raw, kvw, qdw, outw, docw, statw, bias_q, bias_k, gsend, grecv, tsend, trecv,
    x_s, x_r, x_l, kv_s, kv_r, qd_s, qd_r, stat_s, stat_r, out_s, out_r, out_l,
    doc_s, doc_r, gain_s, gain_r, tot_s, tot_r,
):
    me = lax.axis_index("seq")
    row = lax.axis_index("dp")
    side = lax.rem(me, 2)
    level = me // 2
    levels = n_seq // 2
    partner = me + 1 - 2 * side
    chunks = heads // 2
    mine = pl.ds(pl.multiple_of(side * BLOCK, BLOCK), BLOCK)
    theirs = pl.ds(pl.multiple_of((1 - side) * BLOCK, BLOCK), BLOCK)

    def along(dz):
        return lax.rem(me + 2 * dz + n_seq, n_seq)

    def remote(src, dst, send, recv, device):
        return pltpu.make_async_remote_copy(
            src_ref=src, dst_ref=dst, send_sem=send, recv_sem=recv,
            device_id=device, device_id_type=MESH,
        )

    def lanes(h):
        return pl.ds(pl.multiple_of(h * HD, HD), HD)

    def head(c):
        return side * chunks + c

    def other(c):
        return (1 - side) * chunks + c

    sources = (q_ref, k_ref, v_ref, d_ref)
    results = (dq_out, dk_out, dv_out)

    def landing(c, a):
        if a < 2:
            return raw.at[c, a, mine]
        if a == 2:
            return kvw.at[c, REACH, 1, mine]
        return qdw.at[c, 0, 1, mine]

    def swap(c, a):
        return remote(
            sources[a].at[:, lanes(other(c))], landing(c, a), x_s.at[c, a], x_r.at[c, a], {"seq": partner}
        )

    def keep(c, a):
        return pltpu.make_async_copy(sources[a].at[:, lanes(head(c))], landing(c, a), x_l.at[c, a])

    def kv(c, dst):
        return remote(kvw.at[c, dst + 1], kvw.at[c, dst], kv_s.at[c, dst], kv_r.at[c, dst], {"seq": along(1)})

    def qd(c, dst):
        return remote(qdw.at[c, dst - 1], qdw.at[c, dst], qd_s.at[c, dst], qd_r.at[c, dst], {"seq": along(-1)})

    def stat(c, t):
        return remote(statw.at[c, 0], statw.at[c, t], stat_s.at[c, t], stat_r.at[c, t], {"seq": along(-t)})

    def give(c, a):
        return remote(
            outw.at[c, a, theirs], results[a].at[:, lanes(head(c))], out_s.at[c, a], out_r.at[c, a],
            {"seq": partner},
        )

    def put(c, a):
        return pltpu.make_async_copy(outw.at[c, a, mine], results[a].at[:, lanes(head(c))], out_l.at[c, a])

    near = [(dz, flip) for dz in range(-REACH, REACH + 1) for flip in (0, 1) if (dz, flip) != (0, 0)]

    def doc(dz, flip):
        there = side + flip - 2 * side * flip
        target = lax.rem(me - side + there + 2 * dz + n_seq, n_seq)
        slot = 2 * (REACH - dz) + side
        return remote(docw.at[2 * REACH + side], docw.at[slot], doc_s.at[2 * (dz + REACH) + flip],
                      doc_r.at[slot], {"seq": target})

    def doc_arrived(dz, flip):
        there = side + flip - 2 * side * flip
        slot = 2 * (REACH + dz) + there
        return remote(docw.at[slot], docw.at[slot], doc_s.at[slot], doc_r.at[slot], {"seq": partner})

    def gain(c, source):
        return remote(gsend.at[c], grecv.at[source], gain_s.at[c], gain_r.at[source], {"seq": head(c)})

    def total(p, source):
        return remote(tsend, trecv.at[source], tot_s.at[p], tot_r.at[source], {"dp": p})

    barrier = pltpu.get_barrier_semaphore()

    def greet_seq(p, carry):
        @pl.when(p != me)
        def _():
            pl.semaphore_signal(barrier, inc=1, device_id={"seq": p}, device_id_type=MESH)
        return carry

    def greet_dp(p, carry):
        @pl.when(p != row)
        def _():
            pl.semaphore_signal(barrier, inc=1, device_id={"dp": p}, device_id_type=MESH)
        return carry

    lax.fori_loop(0, n_seq, greet_seq, 0)
    lax.fori_loop(0, n_dp, greet_dp, 0)

    def keep_all(c, carry):
        for a in range(4):
            keep(c, a).start()
        return carry

    lax.fori_loop(0, chunks, keep_all, 0)
    docw[2 * REACH + side] = jnp.broadcast_to(doc_ref[...].astype(jnp.float32), (8, BLOCK))
    pl.semaphore_wait(barrier, n_seq - 1 + n_dp - 1)

    def swap_start(c):
        for a in (1, 2, 0, 3):
            swap(c, a).start()

    for c in range(AHEAD):
        swap_start(c)
    for dz, flip in near:
        doc(dz, flip).start()

    def normed(x, gains, h):
        x = x.astype(jnp.float32)
        return (x * inverse_rms(x) * gains[pl.ds(h, 1), :]).astype(jnp.bfloat16)

    def first(c):
        for a in range(4):
            keep(c, a).wait()
        for a in (1, 2):
            swap(c, a).wait_recv()
        kvw[c, REACH, 0] = normed(raw[c, 1], gk_ref, head(c))
        kv(c, 1).start()
        for a in (0, 3):
            swap(c, a).wait_recv()
        qdw[c, 0, 0] = normed(raw[c, 0], gq_ref, head(c))
        qd(c, 1).start()

    def forward(c):
        kv(c, 1).wait_recv()
        kv(c, 0).start()
        qd(c, 1).wait_recv()
        qd(c, 2).start()

    def masks():
        for dz, flip in near:
            doc_arrived(dz, flip).wait_recv()
        rows = lax.broadcasted_iota(jnp.int32, (BLOCK, BLOCK), 0)
        cols = lax.broadcasted_iota(jnp.int32, (BLOCK, BLOCK), 1)
        middle = 2 * REACH
        for sub in range(2):
            own = jnp.broadcast_to(docw[middle + sub, 0:1, :], (BLOCK, BLOCK)).T
            for j in range(5):
                slot = sub + j
                ids = jnp.where(level + slot // 2 - REACH >= 0, docw[slot, 0:1, :], -1.0)
                allowed = own == ids
                if slot == middle + sub:
                    allowed = allowed & (cols <= rows)
                bias_q[sub, :, j * BLOCK:(j + 1) * BLOCK] = jnp.where(allowed, 0.0, MASKED)
                slot = middle + sub + j
                ids = jnp.where(level + slot // 2 - REACH < levels, docw[slot, 0:1, :], -1.0)
                allowed = own == ids
                if j == 0:
                    allowed = allowed & (rows <= cols)
                bias_k[sub, :, j * BLOCK:(j + 1) * BLOCK] = jnp.where(allowed, 0.0, MASKED)

    def norm_back(x, gains, h, grad):
        x = x.astype(jnp.float32)
        rec = inverse_rms(x)
        hat = x * rec
        scaled = grad * gains[pl.ds(h, 1), :]
        back = rec * (scaled - hat * jnp.mean(scaled * hat, axis=-1, keepdims=True))
        return back.astype(jnp.bfloat16), jnp.sum(grad * hat, axis=0, keepdims=True)

    def window(ref, c, a, lo):
        return ref[c, :, a].reshape(SLOTS * PAIR, HD)[lo:lo + SPAN]

    def queries(c):
        kv(c, 0).wait_recv()
        lane = lax.broadcasted_iota(jnp.int32, (BLOCK, BLOCK), 1)
        terms = []
        for sub in range(2):
            lo = sub * BLOCK
            hi = lo + BLOCK
            keys = window(kvw, c, 0, lo)
            s = dot_nt(qdw[c, 0, 0, lo:hi], keys) * (SCALE * LOG2E) + bias_q[sub]
            dprob = dot_nt(qdw[c, 0, 1, lo:hi], window(kvw, c, 1, lo))
            peak = jnp.max(s, axis=1, keepdims=True)
            e = jnp.exp2(s - peak)
            weight = jnp.sum(e, axis=1, keepdims=True)
            inv = 1.0 / weight
            delta = jnp.sum(e * dprob, axis=1, keepdims=True) * inv
            dscore = (e * (inv * SCALE) * (dprob - delta)).astype(jnp.bfloat16)
            grad, term = norm_back(raw[c, 0, lo:hi], gq_ref, head(c), dot_nn(dscore, keys))
            outw[c, 0, lo:hi] = grad
            terms.append(term)
            stats = jnp.where(lane == 0, peak + jnp.log2(weight), delta)
            statw[c, 0, :, lo:hi] = stats.T[0:8]
        for t in range(1, SLOTS):
            stat(c, t).start()
        give(c, 0).start()
        put(c, 0).start()
        gsend[c] = jnp.broadcast_to(terms[0] + terms[1], (8, HD))

    def keys_side(c):
        qd(c, 2).wait_recv()
        for t in range(1, SLOTS):
            stat(c, t).wait_recv()
        lse = jnp.concatenate([statw[c, t, 0:1, :] for t in range(SLOTS)], axis=1)
        delta = jnp.concatenate([statw[c, t, 1:2, :] for t in range(SLOTS)], axis=1)
        terms = []
        for sub in range(2):
            lo = sub * BLOCK
            hi = lo + BLOCK
            qs = window(qdw, c, 0, lo)
            ds = window(qdw, c, 1, lo)
            s = dot_nt(kvw[c, REACH, 0, lo:hi], qs) * (SCALE * LOG2E) + bias_k[sub]
            p = jnp.exp2(s - lse[:, lo:lo + SPAN])
            outw[c, 2, lo:hi] = dot_nn(p.astype(jnp.bfloat16), ds).astype(jnp.bfloat16)
            dprob = dot_nt(kvw[c, REACH, 1, lo:hi], ds)
            dscore = (p * SCALE * (dprob - delta[:, lo:lo + SPAN])).astype(jnp.bfloat16)
            grad, term = norm_back(raw[c, 1, lo:hi], gk_ref, head(c), dot_nn(dscore, qs))
            outw[c, 1, lo:hi] = grad
            terms.append(term)
        gsend[c, 1:2] = terms[0] + terms[1]

        @pl.when(head(c) != me)
        def _():
            gain(c, level).start()

        for a in (1, 2):
            give(c, a).start()
            put(c, a).start()

    def step(t, carry):
        @pl.when(t + AHEAD < chunks)
        def _():
            swap_start(t + AHEAD)

        @pl.when(t < chunks)
        def _():
            first(t)

        @pl.when((t >= FORWARD) & (t < chunks + FORWARD))
        def _():
            forward(t - FORWARD)

        @pl.when(t == FORWARD)
        def _():
            masks()

        @pl.when((t >= QUERIES) & (t < chunks + QUERIES))
        def _():
            queries(t - QUERIES)

        @pl.when((t >= KEYS) & (t < chunks + KEYS))
        def _():
            keys_side(t - KEYS)

        return carry

    lax.fori_loop(0, chunks + KEYS, step, 0)

    owner = me // chunks

    @pl.when(owner == side)
    def _():
        grecv[level] = gsend[me - side * chunks]

    def gain_wait(z, carry):
        @pl.when(2 * z + owner != me)
        def _():
            gain(0, z).wait_recv()
        return carry

    lax.fori_loop(0, levels, gain_wait, 0)
    tsend[...] = jnp.sum(grecv[...], axis=0)
    trecv[row] = tsend[...]

    def total_send(p, carry):
        @pl.when(p != row)
        def _():
            total(p, row).start()
        return carry

    lax.fori_loop(0, n_dp, total_send, 0)

    def drain(c, carry):
        for a in range(4):
            swap(c, a).wait_send()
        for t in range(REACH):
            kv(c, t).wait_send()
            qd(c, t + 1).wait_send()
            stat(c, t + 1).wait_send()
        for a in range(3):
            give(c, a).wait()
            put(c, a).wait()

        @pl.when(head(c) != me)
        def _():
            gain(c, level).wait_send()
        return carry

    lax.fori_loop(0, chunks, drain, 0)
    for dz, flip in near:
        doc(dz, flip).wait_send()

    def total_wait(p, carry):
        @pl.when(p != row)
        def _():
            total(p, p).wait()
        return carry

    lax.fori_loop(0, n_dp, total_wait, 0)
    sums = jnp.sum(trecv[...], axis=0)
    gq_out[...] = sums[0:1]
    gk_out[...] = sums[1:2]


def body(query_states, key_states, value_states, out_grad, doc_ids, query_gain, key_gain):
    n_seq = lax.axis_size("seq")
    n_dp = lax.axis_size("dp")
    rows, feature = query_states.shape[1:]
    heads = feature // HD
    chunks = heads // 2
    window = (chunks, SLOTS, 2, PAIR, HD)
    dma = pltpu.SemaphoreType.DMA
    vmem = pl.BlockSpec(memory_space=pltpu.VMEM)
    anywhere = pl.BlockSpec(memory_space=pl.ANY)
    grad = jax.ShapeDtypeStruct((rows, feature), jnp.bfloat16)
    gain = jax.ShapeDtypeStruct((1, HD), jnp.float32)
    pairs = heads * rows * SPAN
    outs = pl.pallas_call(
        functools.partial(kernel, n_seq, n_dp, heads),
        out_shape=(grad, grad, grad, gain, gain),
        in_specs=[anywhere] * 4 + [vmem] * 3,
        out_specs=(anywhere,) * 3 + (vmem,) * 2,
        scratch_shapes=[
            pltpu.VMEM((chunks, 2, PAIR, HD), jnp.bfloat16),
            pltpu.VMEM(window, jnp.bfloat16),
            pltpu.VMEM(window, jnp.bfloat16),
            pltpu.VMEM((chunks, 3, PAIR, HD), jnp.bfloat16),
            pltpu.VMEM((4 * REACH + 2, 8, BLOCK), jnp.float32),
            pltpu.VMEM((chunks, SLOTS, 8, PAIR), jnp.float32),
            pltpu.VMEM((2, BLOCK, SPAN), jnp.float32),
            pltpu.VMEM((2, BLOCK, SPAN), jnp.float32),
            pltpu.VMEM((chunks, 8, HD), jnp.float32),
            pltpu.VMEM((n_seq // 2, 8, HD), jnp.float32),
            pltpu.VMEM((8, HD), jnp.float32),
            pltpu.VMEM((n_dp, 8, HD), jnp.float32),
            dma((chunks, 4)), dma((chunks, 4)), dma((chunks, 4)),
            dma((chunks, SLOTS)), dma((chunks, SLOTS)),
            dma((chunks, SLOTS)), dma((chunks, SLOTS)),
            dma((chunks, SLOTS)), dma((chunks, SLOTS)),
            dma((chunks, 3)), dma((chunks, 3)), dma((chunks, 3)),
            dma((4 * REACH + 2,)), dma((4 * REACH + 2,)),
            dma((chunks,)), dma((n_seq // 2,)),
            dma((n_dp,)), dma((n_dp,)),
        ],
        cost_estimate=pl.CostEstimate(
            flops=14 * pairs * HD, bytes_accessed=7 * rows * feature * 2, transcendentals=2 * pairs
        ),
        compiler_params=pltpu.CompilerParams(
            collective_id=0, has_side_effects=True, vmem_limit_bytes=60 * 1024 * 1024
        ),
    )(
        query_states[0], key_states[0], value_states[0], out_grad[0], doc_ids,
        query_gain.reshape(heads, HD), key_gain.reshape(heads, HD),
    )
    dq, dk, dv, gq, gk = outs
    return (dq[None], dk[None], dv[None], gq[0], gk[0])


def solution(mesh):
    split = P("dp", "seq", None)
    return jax.shard_map(
        body,
        mesh=mesh,
        in_specs=(split, split, split, split, P("dp", "seq"), P(), P()),
        out_specs=(split, split, split, P("seq"), P("seq")),
        check_vma=False,
    )
```

time: 133 us -> 89.5 us (0.67)
  Pallas kernels: 123 us -> 82.7 us
  local copies, waits for them, and re-layouts: 8.95 us -> 5.1 us
    pallas_call x1, Pallas kernels: 123 us -> 82.7 us  [body(): pl.pallas_call(functools.partial(kernel, n_seq, n_dp, heads), out_shape=(...]
    unnamed x19 -> x13, local copies, waits for them, and re-layouts: 8.95 us -> 5.1 us
where the time goes in v2:
time: 89.5 us; the launch traced here: 88.5 us
  Pallas kernels  82.7 us (92%)
  local copies, waits for them, and re-layouts  5.1 us (6%)
    pallas_call x1, Pallas kernels, body(): pl.pallas_call(functools.partial(kernel, n_seq, n_dp, heads), out_shape=(...  82.7 us
    unnamed x13, local copies, waits for them, and re-layouts  5.1 us

profile of v2, /device:TPU:1, one launch (start us, length us, event | category | flops | bytes accessed | tf_op | source)
XLA Modules:
  0.0 88.5 jit_solution(833284337350429616)
XLA Ops:
  0.6 82.7 %shard_map.110 = (bf16[128,2048]{1,0:T(8,128)(2,1)}, bf16[128,2048]{1,0:T(8,128)(2,1)}, bf16[128,2048]{1,0:T(8,128)(2,1)}, f32[1,128]{1,0:T(1,128)}, f32[1,128]{1,0:T(1,128)}) custom-call(bf16[128,2048]{1,0:T(8,128)(2,1)} %bitcast.14, bf16[128,2048]{1,0:T(8,128)(2,1)} %bitcast.15, bf16[128,2048]{1,0:T(8,128)(2,1)} %bitcast.16, bf16[128,2048]{1,0:T(8,128)(2,1)} %bitcast.17, ...), custom_call_target="tpu_custom_call" | custom-call | flops 2348810240 | bytes 3670016 | tf_op jit(solution)/shard_map/pallas_call | solution.py:374
  83.4 0.0 copy-start.1
  83.4 1.9 %copy.17 = bf16[1,128,2048]{2,1,0:T(8,128)(2,1)} copy(bf16[1,128,2048]{2,1,0:T(8,128)(2,1)} %bitcast.13) | data formatting | bytes 1048576
  85.3 0.0 copy-done.1
  85.3 0.0 copy-start
  85.3 0.8 copy.18
  86.1 0.4 copy-done
  86.6 0.0 copy-start.3
  86.6 0.8 copy.19
  87.3 0.0 copy-done.3
  87.4 0.0 copy-start.2
  87.4 0.5 copy.20
  87.9 0.1 copy-done.2
  88.0 0.5 copy.21
Async XLA Ops:
  83.4 2.0 %copy-start.1 = (bf16[128,2048]{1,0:T(8,128)(2,1)S(1)}, bf16[128,2048]{1,0:T(8,128)(2,1)}, u32[]{:S(2)}) copy-start(bf16[128,2048]{1,0:T(8,128)(2,1)} %get-tuple-element.11) | copy-start | bytes 1572868
  85.3 1.2 %copy-start = (bf16[128,2048]{1,0:T(8,128)(2,1)S(1)}, bf16[128,2048]{1,0:T(8,128)(2,1)}, u32[]{:S(2)}) copy-start(bf16[128,2048]{1,0:T(8,128)(2,1)} %get-tuple-element.12) | copy-start | bytes 1572868
  86.6 0.8 copy-start.3
  87.4 0.6 copy-start.2

commit v3 on v2

--- a/solution.py
+++ b/solution.py
@@ -19,7 +19,7 @@
 SLOTS = REACH + 1
 SPAN = 5 * BLOCK
 MESH = pl.DeviceIdType.MESH
-AHEAD, FORWARD, QUERIES, KEYS = 2, 1, 2, 3
+AHEAD, EARLY, FORWARD, QUERIES, KEYS = 4, 4, 2, 3, 5
 
 
 def dot_nt(a, b):
@@ -36,11 +36,11 @@
 
 def kernel(
     n_seq, n_dp, heads,
-    q_ref, k_ref, v_ref, d_ref, doc_ref, gq_ref, gk_ref,
+    q_ref, k_ref, v_ref, d_ref, doc_any, gq_any, gk_any,
     dq_out, dk_out, dv_out, gq_out, gk_out,
-    raw, kvw, qdw, outw, docw, statw, bias_q, bias_k, gsend, grecv, tsend, trecv,
+    gq_ref, gk_ref, doc_ref, raw, kvw, qdw, outw, docw, statw, bias_q, bias_k, gsend, grecv, tsend, trecv,
     x_s, x_r, x_l, kv_s, kv_r, qd_s, qd_r, stat_s, stat_r, out_s, out_r, out_l,
-    doc_s, doc_r, gain_s, gain_r, tot_s, tot_r,
+    doc_s, doc_r, gain_s, gain_r, tot_s, tot_r, small_s,
 ):
     me = lax.axis_index("seq")
     row = lax.axis_index("dp")
@@ -88,11 +88,19 @@
     def keep(c, a):
         return pltpu.make_async_copy(sources[a].at[:, lanes(head(c))], landing(c, a), x_l.at[c, a])
 
-    def kv(c, dst):
-        return remote(kvw.at[c, dst + 1], kvw.at[c, dst], kv_s.at[c, dst], kv_r.at[c, dst], {"seq": along(1)})
-
-    def qd(c, dst):
-        return remote(qdw.at[c, dst - 1], qdw.at[c, dst], qd_s.at[c, dst], qd_r.at[c, dst], {"seq": along(-1)})
+    def kv(c):
+        return remote(kvw.at[c, 1], kvw.at[c, 0], kv_s.at[c, 2], kv_r.at[c, 2], {"seq": along(1)})
+
+    def qd(c):
+        return remote(qdw.at[c, 1], qdw.at[c, 2], qd_s.at[c, 2], qd_r.at[c, 2], {"seq": along(-1)})
+
+    def kv_half(c, i):
+        half = (mine, theirs)[i]
+        return remote(kvw.at[c, 2, :, half], kvw.at[c, 1, :, half], kv_s.at[c, i], kv_r.at[c, i], {"seq": along(1)})
+
+    def qd_half(c, i):
+        half = (mine, theirs)[i]
+        return remote(qdw.at[c, 0, :, half], qdw.at[c, 1, :, half], qd_s.at[c, i], qd_r.at[c, i], {"seq": along(-1)})
 
     def stat(c, t):
         return remote(statw.at[c, 0], statw.at[c, t], stat_s.at[c, t], stat_r.at[c, t], {"seq": along(-t)})
@@ -128,64 +136,75 @@
 
     barrier = pltpu.get_barrier_semaphore()
 
-    def greet_seq(p, carry):
-        @pl.when(p != me)
-        def _():
-            pl.semaphore_signal(barrier, inc=1, device_id={"seq": p}, device_id_type=MESH)
-        return carry
-
-    def greet_dp(p, carry):
-        @pl.when(p != row)
-        def _():
-            pl.semaphore_signal(barrier, inc=1, device_id={"dp": p}, device_id_type=MESH)
-        return carry
-
-    lax.fori_loop(0, n_seq, greet_seq, 0)
-    lax.fori_loop(0, n_dp, greet_dp, 0)
+    for o in range(1, n_seq):
+        pl.semaphore_signal(barrier, inc=1, device_id={"seq": lax.rem(me + o, n_seq)}, device_id_type=MESH)
+    for o in range(1, n_dp):
+        pl.semaphore_signal(barrier, inc=1, device_id={"dp": lax.rem(row + o, n_dp)}, device_id_type=MESH)
+    small = [
+        pltpu.make_async_copy(src, dst, small_s.at[i])
+        for i, (src, dst) in enumerate(((gq_any, gq_ref), (gk_any, gk_ref), (doc_any, doc_ref)))
+    ]
+    for copy in small:
+        copy.start()
 
     def keep_all(c, carry):
         for a in range(4):
             keep(c, a).start()
         return carry
 
-    lax.fori_loop(0, chunks, keep_all, 0)
-    docw[2 * REACH + side] = jnp.broadcast_to(doc_ref[...].astype(jnp.float32), (8, BLOCK))
-    pl.semaphore_wait(barrier, n_seq - 1 + n_dp - 1)
+    def normed(x, gains, h):
+        x = x.astype(jnp.float32)
+        return (x * inverse_rms(x) * gains[pl.ds(h, 1), :]).astype(jnp.bfloat16)
+
+    def norm_half(c, half):
+        kvw[c, REACH, 0, half] = normed(raw[c, 1, half], gk_ref, head(c))
+        qdw[c, 0, 0, half] = normed(raw[c, 0, half], gq_ref, head(c))
+
+    def mine_ready(c):
+        for a in range(4):
+            keep(c, a).wait()
+        norm_half(c, mine)
+
+    def send_half(c, i):
+        kv_half(c, i).start()
+        qd_half(c, i).start()
 
     def swap_start(c):
         for a in (1, 2, 0, 3):
             swap(c, a).start()
 
+    lax.fori_loop(0, chunks, keep_all, 0)
+    for copy in small:
+        copy.wait()
+    docw[2 * REACH + side] = jnp.broadcast_to(doc_ref[...].astype(jnp.float32), (8, BLOCK))
+    for c in range(EARLY):
+        mine_ready(c)
+    pl.semaphore_wait(barrier, n_seq - 1 + n_dp - 1)
     for c in range(AHEAD):
         swap_start(c)
+    for c in range(EARLY):
+        send_half(c, 0)
     for dz, flip in near:
         doc(dz, flip).start()
 
-    def normed(x, gains, h):
-        x = x.astype(jnp.float32)
-        return (x * inverse_rms(x) * gains[pl.ds(h, 1), :]).astype(jnp.bfloat16)
-
-    def first(c):
+    def rest(c):
         for a in range(4):
-            keep(c, a).wait()
-        for a in (1, 2):
             swap(c, a).wait_recv()
-        kvw[c, REACH, 0] = normed(raw[c, 1], gk_ref, head(c))
-        kv(c, 1).start()
-        for a in (0, 3):
-            swap(c, a).wait_recv()
-        qdw[c, 0, 0] = normed(raw[c, 0], gq_ref, head(c))
-        qd(c, 1).start()
+        norm_half(c, theirs)
+        send_half(c, 1)
 
     def forward(c):
-        kv(c, 1).wait_recv()
-        kv(c, 0).start()
-        qd(c, 1).wait_recv()
-        qd(c, 2).start()
+        for i in range(2):
+            kv_half(c, i).wait_recv()
+        kv(c).start()
+        for i in range(2):
+            qd_half(c, i).wait_recv()
+        qd(c).start()
 
     def masks():
         for dz, flip in near:
             doc_arrived(dz, flip).wait_recv()
+            doc(dz, flip).wait_send()
         rows = lax.broadcasted_iota(jnp.int32, (BLOCK, BLOCK), 0)
         cols = lax.broadcasted_iota(jnp.int32, (BLOCK, BLOCK), 1)
         middle = 2 * REACH
@@ -217,7 +236,7 @@
         return ref[c, :, a].reshape(SLOTS * PAIR, HD)[lo:lo + SPAN]
 
     def queries(c):
-        kv(c, 0).wait_recv()
+        kv(c).wait_recv()
         lane = lax.broadcasted_iota(jnp.int32, (BLOCK, BLOCK), 1)
         terms = []
         for sub in range(2):
@@ -244,7 +263,7 @@
         gsend[c] = jnp.broadcast_to(terms[0] + terms[1], (8, HD))
 
     def keys_side(c):
-        qd(c, 2).wait_recv()
+        qd(c).wait_recv()
         for t in range(1, SLOTS):
             stat(c, t).wait_recv()
         lse = jnp.concatenate([statw[c, t, 0:1, :] for t in range(SLOTS)], axis=1)
@@ -273,6 +292,28 @@
             give(c, a).start()
             put(c, a).start()
 
+    def sent_early(c):
+        for a in range(4):
+            swap(c, a).wait_send()
+        for i in range(2):
+            kv_half(c, i).wait_send()
+            qd_half(c, i).wait_send()
+        kv(c).wait_send()
+        qd(c).wait_send()
+        stat(c, 1).wait_send()
+        stat(c, 2).wait_send()
+        give(c, 0).wait()
+        put(c, 0).wait()
+
+    def sent_late(c):
+        for a in (1, 2):
+            give(c, a).wait()
+            put(c, a).wait()
+
+        @pl.when(head(c) != me)
+        def _():
+            gain(c, level).wait_send()
+
     def step(t, carry):
         @pl.when(t + AHEAD < chunks)
         def _():
@@ -280,7 +321,12 @@
 
         @pl.when(t < chunks)
         def _():
-            first(t)
+            rest(t)
+
+        @pl.when(t + EARLY < chunks)
+        def _():
+            mine_ready(t + EARLY)
+            send_half(t + EARLY, 0)
 
         @pl.when((t >= FORWARD) & (t < chunks + FORWARD))
         def _():
@@ -290,13 +336,18 @@
         def _():
             masks()
 
+        @pl.when((t >= KEYS) & (t < chunks + KEYS))
+        def _():
+            keys_side(t - KEYS)
+
         @pl.when((t >= QUERIES) & (t < chunks + QUERIES))
         def _():
             queries(t - QUERIES)
 
-        @pl.when((t >= KEYS) & (t < chunks + KEYS))
-        def _():
-            keys_side(t - KEYS)
+        @pl.when((t > KEYS) & (t < chunks + KEYS))
+        def _():
+            sent_early(t - KEYS - 1)
+            sent_late(t - KEYS - 1)
 
         return carry
 
@@ -326,26 +377,9 @@
 
     lax.fori_loop(0, n_dp, total_send, 0)
 
-    def drain(c, carry):
-        for a in range(4):
-            swap(c, a).wait_send()
-        for t in range(REACH):
-            kv(c, t).wait_send()
-            qd(c, t + 1).wait_send()
-            stat(c, t + 1).wait_send()
-        for a in range(3):
-            give(c, a).wait()
-            put(c, a).wait()
-
-        @pl.when(head(c) != me)
-        def _():
-            gain(c, level).wait_send()
-        return carry
-
-    lax.fori_loop(0, chunks, drain, 0)
-    for dz, flip in near:
-        doc(dz, flip).wait_send()
-
+    for c in range(chunks - 1, chunks):
+        sent_early(c)
+        sent_late(c)
     def total_wait(p, carry):
         @pl.when(p != row)
         def _():
@@ -356,6 +390,32 @@
     sums = jnp.sum(trecv[...], axis=0)
     gq_out[...] = sums[0:1]
     gk_out[...] = sums[1:2]
+
+
+def hand_over(arrays):
+    n = len(arrays)
+
+    def move(*refs):
+        sources, targets, rooms, sems = refs[:n], refs[n:2 * n], refs[2 * n:3 * n], refs[3 * n]
+        loads = [pltpu.make_async_copy(sources[i], rooms[i], sems.at[0, i]) for i in range(n)]
+        stores = [pltpu.make_async_copy(rooms[i], targets[i], sems.at[1, i]) for i in range(n)]
+        for load in loads:
+            load.start()
+        for load, store in zip(loads, stores):
+            load.wait()
+            store.start()
+        for store in stores:
+            store.wait()
+
+    anywhere = pl.BlockSpec(memory_space=pl.ANY)
+    return pl.pallas_call(
+        move,
+        out_shape=tuple(jax.ShapeDtypeStruct(a.shape, a.dtype) for a in arrays),
+        in_specs=[anywhere] * n,
+        out_specs=(anywhere,) * n,
+        scratch_shapes=[pltpu.VMEM(a.shape, a.dtype) for a in arrays] + [pltpu.SemaphoreType.DMA((2, n))],
+        compiler_params=pltpu.CompilerParams(vmem_limit_bytes=60 * 1024 * 1024),
+    )(*arrays)
 
 
 def body(query_states, key_states, value_states, out_grad, doc_ids, query_gain, key_gain):
@@ -374,9 +434,12 @@
     outs = pl.pallas_call(
         functools.partial(kernel, n_seq, n_dp, heads),
         out_shape=(grad, grad, grad, gain, gain),
-        in_specs=[anywhere] * 4 + [vmem] * 3,
+        in_specs=[anywhere] * 7,
         out_specs=(anywhere,) * 3 + (vmem,) * 2,
         scratch_shapes=[
+            pltpu.VMEM((heads, HD), jnp.float32),
+            pltpu.VMEM((heads, HD), jnp.float32),
+            pltpu.VMEM((1, BLOCK), jnp.int32),
             pltpu.VMEM((chunks, 2, PAIR, HD), jnp.bfloat16),
             pltpu.VMEM(window, jnp.bfloat16),
             pltpu.VMEM(window, jnp.bfloat16),
@@ -396,7 +459,7 @@
             dma((chunks, 3)), dma((chunks, 3)), dma((chunks, 3)),
             dma((4 * REACH + 2,)), dma((4 * REACH + 2,)),
             dma((chunks,)), dma((n_seq // 2,)),
-            dma((n_dp,)), dma((n_dp,)),
+            dma((n_dp,)), dma((n_dp,)), dma((3,)),
         ],
         cost_estimate=pl.CostEstimate(
             flops=14 * pairs * HD, bytes_accessed=7 * rows * feature * 2, transcendentals=2 * pairs
@@ -408,7 +471,7 @@
         query_states[0], key_states[0], value_states[0], out_grad[0], doc_ids,
         query_gain.reshape(heads, HD), key_gain.reshape(heads, HD),
     )
-    dq, dk, dv, gq, gk = outs
+    dq, dk, dv, gq, gk = hand_over(outs)
     return (dq[None], dk[None], dv[None], gq[0], gk[0])
 
 

time: 89.5 us -> 80.4 us (0.90)
  local copies, waits for them, and re-layouts: 5.1 us -> 0 us
  Pallas kernels: 82.7 us -> 79.1 us
    pallas_call x1, Pallas kernels: 82.7 us -> 76.9 us  [body(): pl.pallas_call(functools.partial(kernel, n_seq, n_dp, heads), out_shape=(...]
    unnamed x13 -> x0, local copies, waits for them, and re-layouts: 5.1 us -> none
    pallas_call x0 -> x1, Pallas kernels: none -> 2.27 us  [hand_over(): pl.pallas_call(move, out_shape=tuple((jax.ShapeDtypeStruct(a.shape, a.dty...]
where the time goes in v3:
time: 80.4 us; the launch traced here: 79.8 us
  Pallas kernels  79.1 us (98%)
    pallas_call x1, Pallas kernels, body(): pl.pallas_call(functools.partial(kernel, n_seq, n_dp, heads), out_shape=(...  76.9 us
    pallas_call x1, Pallas kernels, hand_over(): pl.pallas_call(move, out_shape=tuple((jax.ShapeDtypeStruct(a.shape, a.dty...  2.27 us

profile of v3, /device:TPU:1, one launch (start us, length us, event | category | flops | bytes accessed | tf_op | source)
XLA Modules:
  0.0 79.8 jit_solution(16985402289437682116)
XLA Ops:
  0.6 76.9 %shard_map.110 = (bf16[128,2048]{1,0:T(8,128)(2,1)}, bf16[128,2048]{1,0:T(8,128)(2,1)}, bf16[128,2048]{1,0:T(8,128)(2,1)}, f32[1,128]{1,0:T(1,128)}, f32[1,128]{1,0:T(1,128)}) custom-call(bf16[128,2048]{1,0:T(8,128)(2,1)} %bitcast.11, bf16[128,2048]{1,0:T(8,128)(2,1)} %bitcast.12, bf16[128,2048]{1,0:T(8,128)(2,1)} %bitcast.13, bf16[128,2048]{1,0:T(8,128)(2,1)} %bitcast.14, ...), custom_call_target="tpu_custom_call" | custom-call | flops 2348810240 | bytes 3670016 | tf_op jit(solution)/shard_map/pallas_call | solution.py:434
  77.5 2.3 %shard_map.111 = (bf16[128,2048]{1,0:T(8,128)(2,1)}, bf16[128,2048]{1,0:T(8,128)(2,1)}, bf16[128,2048]{1,0:T(8,128)(2,1)}, f32[1,128]{1,0:T(1,128)}, f32[1,128]{1,0:T(1,128)}) custom-call(bf16[128,2048]{1,0:T(8,128)(2,1)} %get-tuple-element.15.refs_0_, bf16[128,2048]{1,0:T(8,128)(2,1)} %get-tuple-element.16.refs_1_, ...), custom_call_target="tpu_custom_call" | custom-call | tf_op jit(solution)/shard_map/pallas_call | solution.py:411

commit v4 on v3

--- a/solution.py
+++ b/solution.py
@@ -49,8 +49,7 @@
     levels = n_seq // 2
     partner = me + 1 - 2 * side
     chunks = heads // 2
-    mine = pl.ds(pl.multiple_of(side * BLOCK, BLOCK), BLOCK)
-    theirs = pl.ds(pl.multiple_of((1 - side) * BLOCK, BLOCK), BLOCK)
+    mine, theirs = side, 1 - side
 
     def along(dz):
         return lax.rem(me + 2 * dz + n_seq, n_seq)
@@ -75,10 +74,10 @@
 
     def landing(c, a):
         if a < 2:
-            return raw.at[c, a, mine]
+            return raw.at[c, side, a]
         if a == 2:
-            return kvw.at[c, REACH, 1, mine]
-        return qdw.at[c, 0, 1, mine]
+            return kvw.at[c, REACH, side, 1]
+        return qdw.at[c, 0, side, 1]
 
     def swap(c, a):
         return remote(
@@ -96,11 +95,16 @@
 
     def kv_half(c, i):
         half = (mine, theirs)[i]
-        return remote(kvw.at[c, 2, :, half], kvw.at[c, 1, :, half], kv_s.at[c, i], kv_r.at[c, i], {"seq": along(1)})
+        return remote(kvw.at[c, 2, half], kvw.at[c, 1, half], kv_s.at[c, i], kv_r.at[c, i], {"seq": along(1)})
 
     def qd_half(c, i):
         half = (mine, theirs)[i]
-        return remote(qdw.at[c, 0, :, half], qdw.at[c, 1, :, half], qd_s.at[c, i], qd_r.at[c, i], {"seq": along(-1)})
+        return remote(qdw.at[c, 0, half], qdw.at[c, 1, half], qd_s.at[c, i], qd_r.at[c, i], {"seq": along(-1)})
+
+    def own(c, act):
+        for i in range(2):
+            act(kv_half(c, i))
+            act(qd_half(c, i))
 
     def stat(c, t):
         return remote(statw.at[c, 0], statw.at[c, t], stat_s.at[c, t], stat_r.at[c, t], {"seq": along(-t)})
@@ -157,8 +161,8 @@
         return (x * inverse_rms(x) * gains[pl.ds(h, 1), :]).astype(jnp.bfloat16)
 
     def norm_half(c, half):
-        kvw[c, REACH, 0, half] = normed(raw[c, 1, half], gk_ref, head(c))
-        qdw[c, 0, 0, half] = normed(raw[c, 0, half], gq_ref, head(c))
+        kvw[c, REACH, half, 0] = normed(raw[c, half, 1], gk_ref, head(c))
+        qdw[c, 0, half, 0] = normed(raw[c, half, 0], gq_ref, head(c))
 
     def mine_ready(c):
         for a in range(4):
@@ -194,11 +198,8 @@
         send_half(c, 1)
 
     def forward(c):
-        for i in range(2):
-            kv_half(c, i).wait_recv()
+        own(c, lambda copy: copy.wait_recv())
         kv(c).start()
-        for i in range(2):
-            qd_half(c, i).wait_recv()
         qd(c).start()
 
     def masks():
@@ -232,72 +233,75 @@
         back = rec * (scaled - hat * jnp.mean(scaled * hat, axis=-1, keepdims=True))
         return back.astype(jnp.bfloat16), jnp.sum(grad * hat, axis=0, keepdims=True)
 
-    def window(ref, c, a, lo):
-        return ref[c, :, a].reshape(SLOTS * PAIR, HD)[lo:lo + SPAN]
+    def window(ref, c, a, sub):
+        parts = [ref[c, (sub + j) // 2, lax.rem(sub + j, 2), a] for j in range(5)]
+        return jnp.concatenate(parts, axis=0)
 
     def queries(c):
         kv(c).wait_recv()
         lane = lax.broadcasted_iota(jnp.int32, (BLOCK, BLOCK), 1)
-        terms = []
+        terms, key_terms = [], []
         for sub in range(2):
             lo = sub * BLOCK
             hi = lo + BLOCK
-            keys = window(kvw, c, 0, lo)
-            s = dot_nt(qdw[c, 0, 0, lo:hi], keys) * (SCALE * LOG2E) + bias_q[sub]
-            dprob = dot_nt(qdw[c, 0, 1, lo:hi], window(kvw, c, 1, lo))
+            keys = window(kvw, c, 0, sub)
+            s = dot_nt(qdw[c, 0, sub, 0], keys) * (SCALE * LOG2E) + bias_q[sub]
+            dprob = dot_nt(qdw[c, 0, sub, 1], window(kvw, c, 1, sub))
             peak = jnp.max(s, axis=1, keepdims=True)
             e = jnp.exp2(s - peak)
             weight = jnp.sum(e, axis=1, keepdims=True)
             inv = 1.0 / weight
             delta = jnp.sum(e * dprob, axis=1, keepdims=True) * inv
             dscore = (e * (inv * SCALE) * (dprob - delta)).astype(jnp.bfloat16)
-            grad, term = norm_back(raw[c, 0, lo:hi], gq_ref, head(c), dot_nn(dscore, keys))
-            outw[c, 0, lo:hi] = grad
+            grad = dot_nn(dscore, keys)
+            back, term = norm_back(raw[c, sub, 0], gq_ref, head(c), grad)
+            outw[c, 0, sub] = back
             terms.append(term)
+            key_terms.append(jnp.sum(grad * qdw[c, 0, sub, 0].astype(jnp.float32), axis=0, keepdims=True))
             stats = jnp.where(lane == 0, peak + jnp.log2(weight), delta)
             statw[c, 0, :, lo:hi] = stats.T[0:8]
         for t in range(1, SLOTS):
             stat(c, t).start()
+        sublane = lax.broadcasted_iota(jnp.int32, (8, HD), 0)
+        gsend[c] = jnp.where(sublane == 0, terms[0] + terms[1], key_terms[0] + key_terms[1])
+
+        @pl.when(head(c) != me)
+        def _():
+            gain(c, level).start()
+
         give(c, 0).start()
         put(c, 0).start()
-        gsend[c] = jnp.broadcast_to(terms[0] + terms[1], (8, HD))
 
     def keys_side(c):
         qd(c).wait_recv()
         for t in range(1, SLOTS):
             stat(c, t).wait_recv()
-        lse = jnp.concatenate([statw[c, t, 0:1, :] for t in range(SLOTS)], axis=1)
-        delta = jnp.concatenate([statw[c, t, 1:2, :] for t in range(SLOTS)], axis=1)
-        terms = []
-        for sub in range(2):
-            lo = sub * BLOCK
-            hi = lo + BLOCK
-            qs = window(qdw, c, 0, lo)
-            ds = window(qdw, c, 1, lo)
-            s = dot_nt(kvw[c, REACH, 0, lo:hi], qs) * (SCALE * LOG2E) + bias_k[sub]
-            p = jnp.exp2(s - lse[:, lo:lo + SPAN])
-            outw[c, 2, lo:hi] = dot_nn(p.astype(jnp.bfloat16), ds).astype(jnp.bfloat16)
-            dprob = dot_nt(kvw[c, REACH, 1, lo:hi], ds)
-            dscore = (p * SCALE * (dprob - delta[:, lo:lo + SPAN])).astype(jnp.bfloat16)
-            grad, term = norm_back(raw[c, 1, lo:hi], gk_ref, head(c), dot_nn(dscore, qs))
-            outw[c, 1, lo:hi] = grad
-            terms.append(term)
-        gsend[c, 1:2] = terms[0] + terms[1]
-
-        @pl.when(head(c) != me)
-        def _():
-            gain(c, level).start()
-
+        def stat_row(r, sub):
+            parts = [
+                statw[c, (sub + j) // 2, r:r + 1, pl.ds(pl.multiple_of(lax.rem(sub + j, 2) * BLOCK, BLOCK), BLOCK)]
+                for j in range(5)
+            ]
+            return jnp.concatenate(parts, axis=1)
+
+        for i, sub in enumerate((theirs, mine)):
+            qs = window(qdw, c, 0, sub)
+            ds = window(qdw, c, 1, sub)
+            s = dot_nt(kvw[c, REACH, sub, 0], qs) * (SCALE * LOG2E) + bias_k[sub]
+            p = jnp.exp2(s - stat_row(0, sub))
+            outw[c, 2, sub] = dot_nn(p.astype(jnp.bfloat16), ds).astype(jnp.bfloat16)
+            dprob = dot_nt(kvw[c, REACH, sub, 1], ds)
+            dscore = (p * SCALE * (dprob - stat_row(1, sub))).astype(jnp.bfloat16)
+            outw[c, 1, sub], _ = norm_back(raw[c, sub, 1], gk_ref, head(c), dot_nn(dscore, qs))
+            if i == 0:
+                for a in (1, 2):
+                    give(c, a).start()
         for a in (1, 2):
-            give(c, a).start()
             put(c, a).start()
 
     def sent_early(c):
         for a in range(4):
             swap(c, a).wait_send()
-        for i in range(2):
-            kv_half(c, i).wait_send()
-            qd_half(c, i).wait_send()
+        own(c, lambda copy: copy.wait_send())
         kv(c).wait_send()
         qd(c).wait_send()
         stat(c, 1).wait_send()
@@ -314,6 +318,31 @@
         def _():
             gain(c, level).wait_send()
 
+    def gains_across():
+        owner = me // chunks
+
+        @pl.when(owner == side)
+        def _():
+            grecv[level] = gsend[me - side * chunks]
+
+        def gain_wait(z, carry):
+            @pl.when(2 * z + owner != me)
+            def _():
+                gain(0, z).wait_recv()
+            return carry
+
+        lax.fori_loop(0, levels, gain_wait, 0)
+        tsend[...] = jnp.sum(grecv[...], axis=0)
+        trecv[row] = tsend[...]
+
+        def total_send(p, carry):
+            @pl.when(p != row)
+            def _():
+                total(p, row).start()
+            return carry
+
+        lax.fori_loop(0, n_dp, total_send, 0)
+
     def step(t, carry):
         @pl.when(t + AHEAD < chunks)
         def _():
@@ -336,6 +365,10 @@
         def _():
             masks()
 
+        @pl.when(t == chunks + QUERIES)
+        def _():
+            gains_across()
+
         @pl.when((t >= KEYS) & (t < chunks + KEYS))
         def _():
             keys_side(t - KEYS)
@@ -353,33 +386,6 @@
 
     lax.fori_loop(0, chunks + KEYS, step, 0)
 
-    owner = me // chunks
-
-    @pl.when(owner == side)
-    def _():
-        grecv[level] = gsend[me - side * chunks]
-
-    def gain_wait(z, carry):
-        @pl.when(2 * z + owner != me)
-        def _():
-            gain(0, z).wait_recv()
-        return carry
-
-    lax.fori_loop(0, levels, gain_wait, 0)
-    tsend[...] = jnp.sum(grecv[...], axis=0)
-    trecv[row] = tsend[...]
-
-    def total_send(p, carry):
-        @pl.when(p != row)
-        def _():
-            total(p, row).start()
-        return carry
-
-    lax.fori_loop(0, n_dp, total_send, 0)
-
-    for c in range(chunks - 1, chunks):
-        sent_early(c)
-        sent_late(c)
     def total_wait(p, carry):
         @pl.when(p != row)
         def _():
@@ -388,8 +394,18 @@
 
     lax.fori_loop(0, n_dp, total_wait, 0)
     sums = jnp.sum(trecv[...], axis=0)
-    gq_out[...] = sums[0:1]
-    gk_out[...] = sums[1:2]
+    sublane = lax.broadcasted_iota(jnp.int32, (8, HD), 0)
+    tsend[...] = jnp.where(sublane == 0, sums, sums / gk_ref[pl.ds(me, 1), :])
+    finals = [
+        pltpu.make_async_copy(tsend.at[0:1], gq_out, small_s.at[0]),
+        pltpu.make_async_copy(tsend.at[1:2], gk_out, small_s.at[1]),
+    ]
+    for copy in finals:
+        copy.start()
+    sent_early(chunks - 1)
+    sent_late(chunks - 1)
+    for copy in finals:
+        copy.wait()
 
 
 def hand_over(arrays):
@@ -424,9 +440,8 @@
     rows, feature = query_states.shape[1:]
     heads = feature // HD
     chunks = heads // 2
-    window = (chunks, SLOTS, 2, PAIR, HD)
+    window = (chunks, SLOTS, 2, 2, BLOCK, HD)
     dma = pltpu.SemaphoreType.DMA
-    vmem = pl.BlockSpec(memory_space=pltpu.VMEM)
     anywhere = pl.BlockSpec(memory_space=pl.ANY)
     grad = jax.ShapeDtypeStruct((rows, feature), jnp.bfloat16)
     gain = jax.ShapeDtypeStruct((1, HD), jnp.float32)
@@ -435,15 +450,15 @@
         functools.partial(kernel, n_seq, n_dp, heads),
         out_shape=(grad, grad, grad, gain, gain),
         in_specs=[anywhere] * 7,
-        out_specs=(anywhere,) * 3 + (vmem,) * 2,
+        out_specs=(anywhere,) * 5,
         scratch_shapes=[
             pltpu.VMEM((heads, HD), jnp.float32),
             pltpu.VMEM((heads, HD), jnp.float32),
             pltpu.VMEM((1, BLOCK), jnp.int32),
-            pltpu.VMEM((chunks, 2, PAIR, HD), jnp.bfloat16),
+            pltpu.VMEM((chunks, 2, 2, BLOCK, HD), jnp.bfloat16),
             pltpu.VMEM(window, jnp.bfloat16),
             pltpu.VMEM(window, jnp.bfloat16),
-            pltpu.VMEM((chunks, 3, PAIR, HD), jnp.bfloat16),
+            pltpu.VMEM((chunks, 3, 2, BLOCK, HD), jnp.bfloat16),
             pltpu.VMEM((4 * REACH + 2, 8, BLOCK), jnp.float32),
             pltpu.VMEM((chunks, SLOTS, 8, PAIR), jnp.float32),
             pltpu.VMEM((2, BLOCK, SPAN), jnp.float32),

time: 80.4 us -> 76.4 us (0.950)
  Pallas kernels: 79.1 us -> 75.6 us
    pallas_call x1, Pallas kernels: 76.9 us -> 73.3 us  [body(): pl.pallas_call(functools.partial(kernel, n_seq, n_dp, heads), out_shape=(...]
where the time goes in v4:
time: 76.4 us; the launch traced here: 76.2 us
  Pallas kernels  75.6 us (99%)
    pallas_call x1, Pallas kernels, body(): pl.pallas_call(functools.partial(kernel, n_seq, n_dp, heads), out_shape=(...  73.3 us
    pallas_call x1, Pallas kernels, hand_over(): pl.pallas_call(move, out_shape=tuple((jax.ShapeDtypeStruct(a.shape, a.dty...  2.27 us

profile of v4, /device:TPU:1, one launch (start us, length us, event | category | flops | bytes accessed | tf_op | source)
XLA Modules:
  0.0 76.2 jit_solution(14087246063815900381)
XLA Ops:
  0.6 73.3 %shard_map.110 = (bf16[128,2048]{1,0:T(8,128)(2,1)}, bf16[128,2048]{1,0:T(8,128)(2,1)}, bf16[128,2048]{1,0:T(8,128)(2,1)}, f32[1,128]{1,0:T(1,128)}, f32[1,128]{1,0:T(1,128)}) custom-call(bf16[128,2048]{1,0:T(8,128)(2,1)} %bitcast.11, bf16[128,2048]{1,0:T(8,128)(2,1)} %bitcast.12, bf16[128,2048]{1,0:T(8,128)(2,1)} %bitcast.13, bf16[128,2048]{1,0:T(8,128)(2,1)} %bitcast.14, ...), custom_call_target="tpu_custom_call" | custom-call | flops 2348810240 | bytes 3670016 | tf_op jit(solution)/shard_map/pallas_call | solution.py:449
  73.9 2.3 %shard_map.111 = (bf16[128,2048]{1,0:T(8,128)(2,1)}, bf16[128,2048]{1,0:T(8,128)(2,1)}, bf16[128,2048]{1,0:T(8,128)(2,1)}, f32[1,128]{1,0:T(1,128)}, f32[1,128]{1,0:T(1,128)}) custom-call(bf16[128,2048]{1,0:T(8,128)(2,1)} %get-tuple-element.15.refs_0_, bf16[128,2048]{1,0:T(8,128)(2,1)} %get-tuple-element.16.refs_1_, ...), custom_call_target="tpu_custom_call" | custom-call | tf_op jit(solution)/shard_map/pallas_call | solution.py:427

commit v5 on v4

--- a/solution.py
+++ b/solution.py
@@ -37,8 +37,9 @@
 def kernel(
     n_seq, n_dp, heads,
     q_ref, k_ref, v_ref, d_ref, doc_any, gq_any, gk_any,
-    dq_out, dk_out, dv_out, gq_out, gk_out,
-    gq_ref, gk_ref, doc_ref, raw, kvw, qdw, outw, docw, statw, bias_q, bias_k, gsend, grecv, tsend, trecv,
+    dq_out, dk_out, dv_out, trecv,
+    gq_ref, gk_ref, doc_ref, raw, kvw, qdw, outw, docw, statw, bias_q, bias_k,
+    score_q, dprob_q, score_k, dprob_k, gsend, grecv, tsend,
     x_s, x_r, x_l, kv_s, kv_r, qd_s, qd_r, stat_s, stat_r, out_s, out_r, out_l,
     doc_s, doc_r, gain_s, gain_r, tot_s, tot_r, small_s,
 ):
@@ -233,37 +234,56 @@
         back = rec * (scaled - hat * jnp.mean(scaled * hat, axis=-1, keepdims=True))
         return back.astype(jnp.bfloat16), jnp.sum(grad * hat, axis=0, keepdims=True)
 
-    def window(ref, c, a, sub):
-        parts = [ref[c, (sub + j) // 2, lax.rem(sub + j, 2), a] for j in range(5)]
+    def window(ref, c, a, sub, start=0, stop=5):
+        parts = [ref[c, (sub + j) // 2, lax.rem(sub + j, 2), a] for j in range(start, stop)]
         return jnp.concatenate(parts, axis=0)
 
+    def queries_early(c):
+        for sub in range(2):
+            start = 2 - sub
+            cols = pl.ds(start * BLOCK, SPAN - start * BLOCK)
+            keys = window(kvw, c, 0, sub, start)
+            s = dot_nt(qdw[c, 0, sub, 0], keys) * (SCALE * LOG2E)
+            score_q[sub, :, cols] = s + bias_q[sub, :, cols]
+            dprob_q[sub, :, cols] = dot_nt(qdw[c, 0, sub, 1], window(kvw, c, 1, sub, start))
+
     def queries(c):
+        queries_early(c)
         kv(c).wait_recv()
         lane = lax.broadcasted_iota(jnp.int32, (BLOCK, BLOCK), 1)
-        terms, key_terms = [], []
+        parts = []
         for sub in range(2):
-            lo = sub * BLOCK
-            hi = lo + BLOCK
-            keys = window(kvw, c, 0, sub)
-            s = dot_nt(qdw[c, 0, sub, 0], keys) * (SCALE * LOG2E) + bias_q[sub]
-            dprob = dot_nt(qdw[c, 0, sub, 1], window(kvw, c, 1, sub))
+            start = 2 - sub
+            cols = pl.ds(0, start * BLOCK)
+            keys = window(kvw, c, 0, sub, 0, start)
+            s = dot_nt(qdw[c, 0, sub, 0], keys) * (SCALE * LOG2E)
+            score_q[sub, :, cols] = s + bias_q[sub, :, cols]
+            dprob_q[sub, :, cols] = dot_nt(qdw[c, 0, sub, 1], window(kvw, c, 1, sub, 0, start))
+            s = score_q[sub]
+            dprob = dprob_q[sub]
             peak = jnp.max(s, axis=1, keepdims=True)
             e = jnp.exp2(s - peak)
             weight = jnp.sum(e, axis=1, keepdims=True)
             inv = 1.0 / weight
             delta = jnp.sum(e * dprob, axis=1, keepdims=True) * inv
-            dscore = (e * (inv * SCALE) * (dprob - delta)).astype(jnp.bfloat16)
-            grad = dot_nn(dscore, keys)
+            stats = jnp.where(lane == 0, peak + jnp.log2(weight), delta)
+            statw[c, 0, :, sub * BLOCK:(sub + 1) * BLOCK] = stats.T[0:8]
+            score_q[sub] = e
+            parts.append((inv, delta))
+        for t in range(1, SLOTS):
+            stat(c, t).start()
+        terms, key_terms = [], []
+        for sub in range(2):
+            inv, delta = parts[sub]
+            dscore = (score_q[sub] * (inv * SCALE) * (dprob_q[sub] - delta)).astype(jnp.bfloat16)
+            grad = dot_nn(dscore, window(kvw, c, 0, sub))
             back, term = norm_back(raw[c, sub, 0], gq_ref, head(c), grad)
             outw[c, 0, sub] = back
             terms.append(term)
             key_terms.append(jnp.sum(grad * qdw[c, 0, sub, 0].astype(jnp.float32), axis=0, keepdims=True))
-            stats = jnp.where(lane == 0, peak + jnp.log2(weight), delta)
-            statw[c, 0, :, lo:hi] = stats.T[0:8]
-        for t in range(1, SLOTS):
-            stat(c, t).start()
         sublane = lax.broadcasted_iota(jnp.int32, (8, HD), 0)
-        gsend[c] = jnp.where(sublane == 0, terms[0] + terms[1], key_terms[0] + key_terms[1])
+        key_term = (key_terms[0] + key_terms[1]) / gk_ref[pl.ds(head(c), 1), :]
+        gsend[c] = jnp.where(sublane == 0, terms[0] + terms[1], key_term)
 
         @pl.when(head(c) != me)
         def _():
@@ -274,8 +294,13 @@
 
     def keys_side(c):
         qd(c).wait_recv()
+        for sub in range(2):
+            s = dot_nt(kvw[c, REACH, sub, 0], window(qdw, c, 0, sub)) * (SCALE * LOG2E)
+            score_k[sub] = s + bias_k[sub]
+            dprob_k[sub] = dot_nt(kvw[c, REACH, sub, 1], window(qdw, c, 1, sub))
         for t in range(1, SLOTS):
             stat(c, t).wait_recv()
+
         def stat_row(r, sub):
             parts = [
                 statw[c, (sub + j) // 2, r:r + 1, pl.ds(pl.multiple_of(lax.rem(sub + j, 2) * BLOCK, BLOCK), BLOCK)]
@@ -284,17 +309,16 @@
             return jnp.concatenate(parts, axis=1)
 
         for i, sub in enumerate((theirs, mine)):
-            qs = window(qdw, c, 0, sub)
-            ds = window(qdw, c, 1, sub)
-            s = dot_nt(kvw[c, REACH, sub, 0], qs) * (SCALE * LOG2E) + bias_k[sub]
-            p = jnp.exp2(s - stat_row(0, sub))
-            outw[c, 2, sub] = dot_nn(p.astype(jnp.bfloat16), ds).astype(jnp.bfloat16)
-            dprob = dot_nt(kvw[c, REACH, sub, 1], ds)
-            dscore = (p * SCALE * (dprob - stat_row(1, sub))).astype(jnp.bfloat16)
-            outw[c, 1, sub], _ = norm_back(raw[c, sub, 1], gk_ref, head(c), dot_nn(dscore, qs))
+            p = jnp.exp2(score_k[sub] - stat_row(0, sub))
+            dv = dot_nn(p.astype(jnp.bfloat16), window(qdw, c, 1, sub))
+            outw[c, 2, sub] = dv.astype(jnp.bfloat16)
             if i == 0:
-                for a in (1, 2):
-                    give(c, a).start()
+                give(c, 2).start()
+            dscore = (p * SCALE * (dprob_k[sub] - stat_row(1, sub))).astype(jnp.bfloat16)
+            grad = dot_nn(dscore, window(qdw, c, 0, sub))
+            outw[c, 1, sub], _ = norm_back(raw[c, sub, 1], gk_ref, head(c), grad)
+            if i == 0:
+                give(c, 1).start()
         for a in (1, 2):
             put(c, a).start()
 
@@ -333,7 +357,7 @@
 
         lax.fori_loop(0, levels, gain_wait, 0)
         tsend[...] = jnp.sum(grecv[...], axis=0)
-        trecv[row] = tsend[...]
+        pltpu.make_async_copy(tsend, trecv.at[row], small_s.at[0]).start()
 
         def total_send(p, carry):
             @pl.when(p != row)
@@ -393,45 +417,46 @@
         return carry
 
     lax.fori_loop(0, n_dp, total_wait, 0)
-    sums = jnp.sum(trecv[...], axis=0)
-    sublane = lax.broadcasted_iota(jnp.int32, (8, HD), 0)
-    tsend[...] = jnp.where(sublane == 0, sums, sums / gk_ref[pl.ds(me, 1), :])
-    finals = [
-        pltpu.make_async_copy(tsend.at[0:1], gq_out, small_s.at[0]),
-        pltpu.make_async_copy(tsend.at[1:2], gk_out, small_s.at[1]),
-    ]
-    for copy in finals:
-        copy.start()
+    pltpu.make_async_copy(tsend, trecv.at[row], small_s.at[0]).wait()
     sent_early(chunks - 1)
     sent_late(chunks - 1)
-    for copy in finals:
-        copy.wait()
-
-
-def hand_over(arrays):
+
+
+def hand_over(arrays, totals):
     n = len(arrays)
 
     def move(*refs):
-        sources, targets, rooms, sems = refs[:n], refs[n:2 * n], refs[2 * n:3 * n], refs[3 * n]
-        loads = [pltpu.make_async_copy(sources[i], rooms[i], sems.at[0, i]) for i in range(n)]
-        stores = [pltpu.make_async_copy(rooms[i], targets[i], sems.at[1, i]) for i in range(n)]
+        sources, totals_ref = refs[:n], refs[n]
+        targets, gains = refs[n + 1:2 * n + 1], refs[2 * n + 1:2 * n + 3]
+        rooms, totals_room, sums, sems = refs[2 * n + 3:3 * n + 3], refs[-3], refs[-2], refs[-1]
+        loads = [pltpu.make_async_copy(totals_ref, totals_room, sems.at[0, n])]
+        loads += [pltpu.make_async_copy(sources[i], rooms[i], sems.at[0, i]) for i in range(n)]
+        stores = [pltpu.make_async_copy(sums.at[i:i + 1], gains[i], sems.at[1, n + i]) for i in range(2)]
+        stores += [pltpu.make_async_copy(rooms[i], targets[i], sems.at[1, i]) for i in range(n)]
         for load in loads:
             load.start()
-        for load, store in zip(loads, stores):
+        loads[0].wait()
+        sums[...] = jnp.sum(totals_room[...], axis=0)
+        for store in stores[:2]:
+            store.start()
+        for load, store in zip(loads[1:], stores[2:]):
             load.wait()
             store.start()
         for store in stores:
             store.wait()
 
     anywhere = pl.BlockSpec(memory_space=pl.ANY)
+    gain = jax.ShapeDtypeStruct((1, HD), jnp.float32)
     return pl.pallas_call(
         move,
-        out_shape=tuple(jax.ShapeDtypeStruct(a.shape, a.dtype) for a in arrays),
-        in_specs=[anywhere] * n,
-        out_specs=(anywhere,) * n,
-        scratch_shapes=[pltpu.VMEM(a.shape, a.dtype) for a in arrays] + [pltpu.SemaphoreType.DMA((2, n))],
+        out_shape=tuple(jax.ShapeDtypeStruct(a.shape, a.dtype) for a in arrays) + (gain, gain),
+        in_specs=[anywhere] * (n + 1),
+        out_specs=(anywhere,) * (n + 2),
+        scratch_shapes=[pltpu.VMEM(a.shape, a.dtype) for a in arrays]
+        + [pltpu.VMEM(totals.shape, totals.dtype), pltpu.VMEM((8, HD), jnp.float32)]
+        + [pltpu.SemaphoreType.DMA((2, n + 2))],
         compiler_params=pltpu.CompilerParams(vmem_limit_bytes=60 * 1024 * 1024),
-    )(*arrays)
+    )(*arrays, totals)
 
 
 def body(query_states, key_states, value_states, out_grad, doc_ids, query_gain, key_gain):
@@ -444,13 +469,13 @@
     dma = pltpu.SemaphoreType.DMA
     anywhere = pl.BlockSpec(memory_space=pl.ANY)
     grad = jax.ShapeDtypeStruct((rows, feature), jnp.bfloat16)
-    gain = jax.ShapeDtypeStruct((1, HD), jnp.float32)
+    totals = jax.ShapeDtypeStruct((n_dp, 8, HD), jnp.float32)
     pairs = heads * rows * SPAN
     outs = pl.pallas_call(
         functools.partial(kernel, n_seq, n_dp, heads),
-        out_shape=(grad, grad, grad, gain, gain),
+        out_shape=(grad, grad, grad, totals),
         in_specs=[anywhere] * 7,
-        out_specs=(anywhere,) * 5,
+        out_specs=(anywhere,) * 4,
         scratch_shapes=[
             pltpu.VMEM((heads, HD), jnp.float32),
             pltpu.VMEM((heads, HD), jnp.float32),
@@ -463,10 +488,13 @@
             pltpu.VMEM((chunks, SLOTS, 8, PAIR), jnp.float32),
             pltpu.VMEM((2, BLOCK, SPAN), jnp.float32),
             pltpu.VMEM((2, BLOCK, SPAN), jnp.float32),
+            pltpu.VMEM((2, BLOCK, SPAN), jnp.float32),
+            pltpu.VMEM((2, BLOCK, SPAN), jnp.float32),
+            pltpu.VMEM((2, BLOCK, SPAN), jnp.float32),
+            pltpu.VMEM((2, BLOCK, SPAN), jnp.float32),
             pltpu.VMEM((chunks, 8, HD), jnp.float32),
             pltpu.VMEM((n_seq // 2, 8, HD), jnp.float32),
             pltpu.VMEM((8, HD), jnp.float32),
-            pltpu.VMEM((n_dp, 8, HD), jnp.float32),
             dma((chunks, 4)), dma((chunks, 4)), dma((chunks, 4)),
             dma((chunks, SLOTS)), dma((chunks, SLOTS)),
             dma((chunks, SLOTS)), dma((chunks, SLOTS)),
@@ -486,7 +514,7 @@
         query_states[0], key_states[0], value_states[0], out_grad[0], doc_ids,
         query_gain.reshape(heads, HD), key_gain.reshape(heads, HD),
     )
-    dq, dk, dv, gq, gk = hand_over(outs)
+    dq, dk, dv, gq, gk = hand_over(outs[:3], outs[3])
     return (dq[None], dk[None], dv[None], gq[0], gk[0])
 
 

time: 76.4 us -> 75.6 us (0.990)
  Pallas kernels: 75.6 us -> 74.8 us
    pallas_call x1, Pallas kernels: 73.3 us -> 72.5 us  [body(): pl.pallas_call(functools.partial(kernel, n_seq, n_dp, heads), out_shape=(...]
where the time goes in v5:
time: 75.6 us; the launch traced here: 75.4 us
  Pallas kernels  74.8 us (99%)
    pallas_call x1, Pallas kernels, body(): pl.pallas_call(functools.partial(kernel, n_seq, n_dp, heads), out_shape=(...  72.5 us
    pallas_call x1, Pallas kernels, hand_over(): pl.pallas_call(move, out_shape=tuple((jax.ShapeDtypeStruct(a.shape, a.dty...  2.31 us

profile of v5, /device:TPU:1, one launch (start us, length us, event | category | flops | bytes accessed | tf_op | source)
XLA Modules:
  0.0 75.4 jit_solution(8031553395126207244)
XLA Ops:
  0.6 72.5 %shard_map.110 = (bf16[128,2048]{1,0:T(8,128)(2,1)}, bf16[128,2048]{1,0:T(8,128)(2,1)}, bf16[128,2048]{1,0:T(8,128)(2,1)}, f32[16,8,128]{2,1,0:T(8,128)}) custom-call(bf16[128,2048]{1,0:T(8,128)(2,1)} %bitcast.11, bf16[128,2048]{1,0:T(8,128)(2,1)} %bitcast.12, bf16[128,2048]{1,0:T(8,128)(2,1)} %bitcast.13, bf16[128,2048]{1,0:T(8,128)(2,1)} %bitcast.14, ...), custom_call_target="tpu_custom_call" | custom-call | flops 2348810240 | bytes 3670016 | tf_op jit(solution)/shard_map/pallas_call | solution.py:474
  73.1 2.3 %shard_map.111 = (bf16[128,2048]{1,0:T(8,128)(2,1)}, bf16[128,2048]{1,0:T(8,128)(2,1)}, bf16[128,2048]{1,0:T(8,128)(2,1)}, f32[1,128]{1,0:T(1,128)}, f32[1,128]{1,0:T(1,128)}) custom-call(bf16[128,2048]{1,0:T(8,128)(2,1)} %get-tuple-element.14.refs_0_, bf16[128,2048]{1,0:T(8,128)(2,1)} %get-tuple-element.15.refs_1_, ...), custom_call_target="tpu_custom_call" | custom-call | tf_op jit(solution)/shard_map/pallas_call | solution.py:450

commit v6 on v5

--- a/solution.py
+++ b/solution.py
@@ -181,7 +181,7 @@
     lax.fori_loop(0, chunks, keep_all, 0)
     for copy in small:
         copy.wait()
-    docw[2 * REACH + side] = jnp.broadcast_to(doc_ref[...].astype(jnp.float32), (8, BLOCK))
+    docw[2 * REACH + side] = doc_ref[...].astype(jnp.float32)
     for c in range(EARLY):
         mine_ready(c)
     pl.semaphore_wait(barrier, n_seq - 1 + n_dp - 1)
@@ -267,7 +267,7 @@
             inv = 1.0 / weight
             delta = jnp.sum(e * dprob, axis=1, keepdims=True) * inv
             stats = jnp.where(lane == 0, peak + jnp.log2(weight), delta)
-            statw[c, 0, :, sub * BLOCK:(sub + 1) * BLOCK] = stats.T[0:8]
+            statw[c, 0, :, sub * BLOCK:(sub + 1) * BLOCK] = stats.T[0:2]
             score_q[sub] = e
             parts.append((inv, delta))
         for t in range(1, SLOTS):
@@ -281,9 +281,8 @@
             outw[c, 0, sub] = back
             terms.append(term)
             key_terms.append(jnp.sum(grad * qdw[c, 0, sub, 0].astype(jnp.float32), axis=0, keepdims=True))
-        sublane = lax.broadcasted_iota(jnp.int32, (8, HD), 0)
-        key_term = (key_terms[0] + key_terms[1]) / gk_ref[pl.ds(head(c), 1), :]
-        gsend[c] = jnp.where(sublane == 0, terms[0] + terms[1], key_term)
+        gsend[c, 0:1] = terms[0] + terms[1]
+        gsend[c, 1:2] = (key_terms[0] + key_terms[1]) / gk_ref[pl.ds(head(c), 1), :]
 
         @pl.when(head(c) != me)
         def _():
@@ -453,7 +452,7 @@
         in_specs=[anywhere] * (n + 1),
         out_specs=(anywhere,) * (n + 2),
         scratch_shapes=[pltpu.VMEM(a.shape, a.dtype) for a in arrays]
-        + [pltpu.VMEM(totals.shape, totals.dtype), pltpu.VMEM((8, HD), jnp.float32)]
+        + [pltpu.VMEM(totals.shape, totals.dtype), pltpu.VMEM((2, HD), jnp.float32)]
         + [pltpu.SemaphoreType.DMA((2, n + 2))],
         compiler_params=pltpu.CompilerParams(vmem_limit_bytes=60 * 1024 * 1024),
     )(*arrays, totals)
@@ -469,7 +468,7 @@
     dma = pltpu.SemaphoreType.DMA
     anywhere = pl.BlockSpec(memory_space=pl.ANY)
     grad = jax.ShapeDtypeStruct((rows, feature), jnp.bfloat16)
-    totals = jax.ShapeDtypeStruct((n_dp, 8, HD), jnp.float32)
+    totals = jax.ShapeDtypeStruct((n_dp, 2, HD), jnp.float32)
     pairs = heads * rows * SPAN
     outs = pl.pallas_call(
         functools.partial(kernel, n_seq, n_dp, heads),
@@ -484,17 +483,17 @@
             pltpu.VMEM(window, jnp.bfloat16),
             pltpu.VMEM(window, jnp.bfloat16),
             pltpu.VMEM((chunks, 3, 2, BLOCK, HD), jnp.bfloat16),
-            pltpu.VMEM((4 * REACH + 2, 8, BLOCK), jnp.float32),
-            pltpu.VMEM((chunks, SLOTS, 8, PAIR), jnp.float32),
+            pltpu.VMEM((4 * REACH + 2, 1, BLOCK), jnp.float32),
+            pltpu.VMEM((chunks, SLOTS, 2, PAIR), jnp.float32),
             pltpu.VMEM((2, BLOCK, SPAN), jnp.float32),
             pltpu.VMEM((2, BLOCK, SPAN), jnp.float32),
             pltpu.VMEM((2, BLOCK, SPAN), jnp.float32),
             pltpu.VMEM((2, BLOCK, SPAN), jnp.float32),
             pltpu.VMEM((2, BLOCK, SPAN), jnp.float32),
             pltpu.VMEM((2, BLOCK, SPAN), jnp.float32),
-            pltpu.VMEM((chunks, 8, HD), jnp.float32),
-            pltpu.VMEM((n_seq // 2, 8, HD), jnp.float32),
-            pltpu.VMEM((8, HD), jnp.float32),
+            pltpu.VMEM((chunks, 2, HD), jnp.float32),
+            pltpu.VMEM((n_seq // 2, 2, HD), jnp.float32),
+            pltpu.VMEM((2, HD), jnp.float32),
             dma((chunks, 4)), dma((chunks, 4)), dma((chunks, 4)),
             dma((chunks, SLOTS)), dma((chunks, SLOTS)),
             dma((chunks, SLOTS)), dma((chunks, SLOTS)),

time: 75.6 us -> 73.2 us (0.968)
  the two profiles are of different devices: /device:TPU:1 before, /device:TPU:96 now
where the time goes in v6:
time: 73.2 us; the launch traced here: 72.9 us
  Pallas kernels  72.3 us (99%)
    pallas_call x1, Pallas kernels, body(): pl.pallas_call(functools.partial(kernel, n_seq, n_dp, heads), out_shape=(...  70 us
    pallas_call x1, Pallas kernels, hand_over(): pl.pallas_call(move, out_shape=tuple((jax.ShapeDtypeStruct(a.shape, a.dty...  2.29 us

profile of v6, /device:TPU:96, one launch (start us, length us, event | category | flops | bytes accessed | tf_op | source)
XLA Modules:
  0.0 72.9 jit_solution(12831812535626401395)
XLA Ops:
  0.6 70.0 %shard_map.110 = (bf16[128,2048]{1,0:T(8,128)(2,1)}, bf16[128,2048]{1,0:T(8,128)(2,1)}, bf16[128,2048]{1,0:T(8,128)(2,1)}, f32[16,2,128]{2,1,0:T(2,128)}) custom-call(bf16[128,2048]{1,0:T(8,128)(2,1)} %bitcast.11, bf16[128,2048]{1,0:T(8,128)(2,1)} %bitcast.12, bf16[128,2048]{1,0:T(8,128)(2,1)} %bitcast.13, bf16[128,2048]{1,0:T(8,128)(2,1)} %bitcast.14, ...), custom_call_target="tpu_custom_call" | custom-call | flops 2348810240 | bytes 3670016 | tf_op jit(solution)/shard_map/pallas_call | solution.py:473
  70.6 2.3 %shard_map.111 = (bf16[128,2048]{1,0:T(8,128)(2,1)}, bf16[128,2048]{1,0:T(8,128)(2,1)}, bf16[128,2048]{1,0:T(8,128)(2,1)}, f32[1,128]{1,0:T(1,128)}, f32[1,128]{1,0:T(1,128)}) custom-call(bf16[128,2048]{1,0:T(8,128)(2,1)} %get-tuple-element.14.refs_0_, bf16[128,2048]{1,0:T(8,128)(2,1)} %get-tuple-element.15.refs_1_, ...), custom_call_target="tpu_custom_call" | custom-call | tf_op jit(solution)/shard_map/pallas_call | solution.py:449
